TPU v7x, 128 devices: a whole 4x4x4 slice. The times are simulated.
128 devices in a mesh: row: 8 (over z, core), col: 16 (over x, y).
Axes of the slice: x: 4, y: 4, z: 4, core: 2. Of those that a mesh axis runs over, the one named last changes fastest.
Arguments:
- basis_values: bfloat16 [128, 1536, 1024], P(('row', 'col')), may hold values from -6 to 6
- quad_weights: float32 [128, 1536], P(('row', 'col')), may hold values from 0.0001953125 to 0.001953125
- point_counts: int32 [128], P(('row', 'col')), may hold values from 192 to 1536, as said below
- basis_tiles: int32 [128, 8], replicated, may hold values from 0 to 47, as said below
- density: bfloat16 [6144, 6144], P('row', 'col'), may hold values from -0.005859375 to 0.005859375
- core_matrix: float32 [6144, 6144], P('row', 'col'), as said below
- map_shift: float32 [1], replicated, may hold values from 0.2 to 0.6
- map_scale: float32 [1], replicated, may hold values from -0.05 to -0.03
- branch_flags: int32 [1], replicated, may hold values from 0 to 1
Outputs:
- point_density: float32 [128, 1536], P(('row', 'col'))
- xc_potential: float32 [6144, 6144], P('row', 'col')
- purified: float32 [6144, 6144], P('row', 'col')
Inputs may be any that keep to these rules, and one draw needn't show every extreme that they name: `basis_tiles`: entry j of every row lies in j * 6 to (j + 1) * 6 - 1. The first point_counts[q] points of batch q are live; some batch has all 1536 live. `core_matrix`: a symmetric matrix.
All inputs are finite; a program needn't handle non-finite values.
Results may differ from a plain program's by a relative error of at most 0.0067.
Values may be sent and summed in bfloat16 or wider, within the bound.
A program may use at most 64 MiB of HBM per device.

v0:
```python
import jax
import jax.numpy as jnp
from jax import lax
from jax.sharding import PartitionSpec as P

TILE = 128


SLATER = (3.0 / 3.141592653589793) ** (1.0 / 3.0)


def potential_factor(values):
    return -SLATER * (values * values + 1.0) ** (1.0 / 6.0)


def body(
    basis_values,
    quad_weights,
    point_counts,
    basis_tiles,
    density,
    core_matrix,
    map_shift,
    map_scale,
    branch_flags,
):
    row_count = lax.axis_size("row")
    col_count = lax.axis_size("col")
    devices_all = row_count * col_count
    row_index = lax.axis_index("row")
    col_index = lax.axis_index("col")
    local_rows, local_cols = density.shape
    band_rows = local_rows // TILE
    band_cols = local_cols // TILE
    per_device = basis_values.shape[0]
    batch_total = basis_tiles.shape[0]
    points = basis_values.shape[1]
    width = basis_values.shape[2]
    blocks = width // TILE
    block_span = band_rows * row_count // blocks
    slots_row = max(1, band_rows // block_span)
    slots_col = max(1, band_cols // block_span)
    first_row = row_index * band_rows // block_span
    first_col = col_index * band_cols // block_span
    wanted_rows = jnp.take(basis_tiles, first_row + jnp.arange(slots_row, dtype=jnp.int32), axis=1)
    wanted_cols = jnp.take(basis_tiles, first_col + jnp.arange(slots_col, dtype=jnp.int32), axis=1)
    owned = (wanted_rows // band_rows == row_index)[:, :, None] & (
        wanted_cols // band_cols == col_index
    )[:, None, :]
    local_row = jnp.clip(wanted_rows - row_index * band_rows, 0, band_rows - 1)
    local_col = jnp.clip(wanted_cols - col_index * band_cols, 0, band_cols - 1)
    tile_grid = density.reshape(band_rows, TILE, band_cols, TILE).transpose(0, 2, 1, 3)
    outgoing = tile_grid[local_row[:, :, None], local_col[:, None, :]]
    outgoing = jnp.where(owned[:, :, :, None, None], outgoing, jnp.zeros((), jnp.bfloat16))
    outgoing = outgoing.reshape(devices_all, per_device, slots_row, slots_col, TILE, TILE)
    arrived = lax.all_to_all(outgoing, ("row", "col"), split_axis=0, concat_axis=0, tiled=True)
    my_start = (row_index * col_count + col_index) * per_device
    my_tiles = lax.dynamic_slice_in_dim(basis_tiles, my_start, per_device, 0)
    owner_row = my_tiles // band_rows
    owner_col = my_tiles // band_cols
    source = owner_row[:, :, None] * col_count + owner_col[:, None, :]
    block_ids = jnp.arange(blocks, dtype=jnp.int32)[None, :]
    slot_row = block_ids - owner_row * band_rows // block_span
    slot_col = block_ids - owner_col * band_cols // block_span
    batch_slot = jnp.arange(per_device, dtype=jnp.int32)[:, None, None]
    gathered = arrived[source, batch_slot, slot_row[:, :, None], slot_col[:, None, :]]
    submatrix = gathered.transpose(0, 1, 3, 2, 4).reshape(per_device, width, width)
    point_ids = jnp.arange(points, dtype=jnp.int32)
    values = basis_values[0]
    mixed = jnp.dot(values, submatrix[0], preferred_element_type=jnp.float32)
    local_density = jnp.sum(mixed * values.astype(jnp.float32), axis=1)
    live = point_ids < point_counts[0]
    local_density = jnp.where(live, local_density, jnp.float32(0.0))
    factor = jnp.where(live, quad_weights[0] * potential_factor(local_density), jnp.float32(0.0))
    weighted = (factor[:, None] * values).astype(jnp.bfloat16)
    contributions = [jnp.dot(values.T, weighted, preferred_element_type=jnp.float32)]
    densities = [local_density]
    block_tiles = (
        jnp.stack(contributions)
        .reshape(per_device, blocks, TILE, blocks, TILE)
        .transpose(0, 1, 3, 2, 4)
    )
    returning = jnp.zeros((devices_all, per_device, slots_row, slots_col, TILE, TILE), jnp.float32)
    returning = returning.at[source, batch_slot, slot_row[:, :, None], slot_col[:, None, :]].set(
        block_tiles
    )
    landed = lax.all_to_all(returning, ("row", "col"), split_axis=0, concat_axis=0, tiled=True)
    landed = landed.reshape(batch_total, slots_row, slots_col, TILE, TILE)
    landed = jnp.where(owned[:, :, :, None, None], landed, jnp.float32(0.0))
    row_target = local_row[:, :, None]
    col_target = local_col[:, None, :]
    summed = (
        jnp.zeros((band_rows, band_cols, TILE, TILE), jnp.float32)
        .at[row_target, col_target]
        .add(landed)
    )
    potential = summed.transpose(0, 2, 1, 3).reshape(local_rows, local_cols)
    global_rows = row_index * local_rows + jnp.arange(local_rows, dtype=jnp.int32)
    global_cols = col_index * local_cols + jnp.arange(local_cols, dtype=jnp.int32)
    identity = (global_rows[:, None] == global_cols[None, :]).astype(jnp.float32)
    start = map_shift[0] * identity + map_scale[0] * (core_matrix + potential)
    rounded = start.astype(jnp.bfloat16)
    column_block = lax.all_gather(rounded, "row", axis=0, tiled=True)
    square = jnp.dot(
        lax.all_gather(rounded, "col", axis=1, tiled=True),
        column_block,
        preferred_element_type=jnp.float32,
    )
    purified = jnp.where(branch_flags[0] == 0, square, 2.0 * start - square)
    return (jnp.stack(densities), potential, purified)


def solution(mesh):
    placed = (
        P(("row", "col"), None, None),
        P(("row", "col"), None),
        P(("row", "col")),
        P(),
        P("row", "col"),
        P("row", "col"),
        P(),
        P(),
        P(),
    )
    return jax.shard_map(
        body,
        mesh=mesh,
        in_specs=placed,
        out_specs=(P(("row", "col"), None), P("row", "col"), P("row", "col")),
        check_vma=False,
    )
```

profile of v0, /device:TPU:0, one launch (start us, length us, event | category | flops | bytes accessed | tf_op | source)
XLA Modules:
  0.0 394.2 jit_solution(7734751450457148408)
XLA Ops:
  7.2 0.8 compare_select_fusion.5
  8.0 0.8 and_bitcast_fusion
  8.8 2.0 reshape.423
  10.8 0.1 copy.46
  11.0 3.1 gather_fusion
  14.1 4.5 %fusion.2 = bf16[128,1,1,1,128,128]{5,4,3,2,1,0:T(8,128)(2,1)} fusion(bf16[128,128,128]{2,1,0:T(8,128)(2,1)} %gather_fusion, pred[128]{0:T(512)(128)(4,1)S(1)} %and_bitcast_fusion), kind=kLoop, calls=%fused_computation.10 | loop fusion | flops 2097152 | bytes 8388736 | tf_op jit(solution)/shard_map/jit(_where)/select_n | solution.py:54
  18.6 0.0 copy-start.3
  18.6 11.9 %all-to-all-start = ((bf16[128,1,1,1,128,128]{5,4,3,2,1,0:T(8,128)(2,1)}), bf16[128,1,1,1,128,128]{5,4,3,2,1,0:T(8,128)(2,1)}, u32[]{:S(2)}, u32[]{:S(2)}) async-start(bf16[128,1,1,1,128,128]{5,4,3,2,1,0:T(8,128)(2,1)} %fusion.2), calls=%async_computation | async-start | bytes 8388608 | tf_op jit(solution)/shard_map/all_to_all | solution.py:56
  30.5 0.0 copy-done.3
  30.5 0.2 multiply_reduce_fusion
  30.7 0.1 compare_select_fusion.1
  30.8 0.1 broadcast_in_dim.61
  30.9 0.1 reshape.391
  31.0 0.0 copy-start.4
  31.0 4.7 %copy.26 = bf16[1,1536,1024]{1,2,0:T(8,128)(2,1)} copy(bf16[1,1536,1024]{2,1,0:T(8,128)(2,1)} %param.11) | data formatting | bytes 6291456 | tf_op args[0]
  36.3 0.1 reshape.403
  36.4 0.0 copy-done.4
  36.5 45.0 %all-to-all-done = bf16[128,1,1,1,128,128]{5,4,3,2,1,0:T(8,128)(2,1)} async-done(((bf16[128,1,1,1,128,128]{5,4,3,2,1,0:T(8,128)(2,1)}), bf16[128,1,1,1,128,128]{5,4,3,2,1,0:T(8,128)(2,1)}, u32[]{:S(2)}, u32[]{:S(2)}) %all-to-all-start) | async-done | bytes 4194336 | tf_op jit(solution)/shard_map/all_to_all | solution.py:56
  81.5 3.1 gather_fusion.1
  84.6 0.0 copy-start
  84.6 1.4 copy.25
  86.0 0.5 copy-done
  86.5 5.3 %fusion.1 = f32[1536]{0:T(1024)S(1)} fusion(bf16[1,1536,1024]{2,1,0:T(8,128)(2,1)S(1)} %copy-done, bf16[1,1536,1024]{1,2,0:T(8,128)(2,1)} %copy.26, bf16[128,8,8,128]{3,2,1,0:T(8,128)(2,1)S(1)} %bitcast.103), kind=kOutput, calls=%fused_computation.7 | convolution fusion | flops 3225942528 | bytes 8394752 | tf_op jit(solution)/shard_map/dot_general | solution.py:70
  91.8 3.7 fusion.9
  95.5 3.0 copy.37
  98.5 5.4 %copy.27 = f32[1,8,128,8,128]{4,2,3,1,0:T(8,128)} copy(f32[1,8,128,8,128]{2,1,4,3,0:T(8,128)} %bitcast.99) | data formatting | bytes 8388608 | tf_op jit(solution)/shard_map/reshape;stack | solution.py:80
  103.9 4.3 %broadcast.385 = f32[128,128,128]{2,1,0:T(8,128)} broadcast(f32[]{:T(128)} %constant.94.clone.1), dimensions={} | broadcast | bytes 8388612 | tf_op jit(solution)/shard_map/broadcast_in_dim | solution.py:83
  108.2 12.0 %scatter_fusion = f32[128,128,128]{2,1,0:T(8,128)} fusion(f32[128,128,128]{2,1,0:T(8,128)} %broadcast.385, s32[64]{0:T(128)S(1)} %reshape.403, f32[64,128,128]{2,1,0:T(8,128)} %bitcast.98), kind=kCustom, calls=%fused_computation.2 | custom fusion | bytes 12583168 | tf_op jit(solution)/shard_map/scatter | solution.py:84
  120.2 5.9 %all-to-all-start.1 = ((f32[128,1,1,1,128,128]{5,4,3,2,1,0:T(8,128)}), f32[128,1,1,1,128,128]{5,4,3,2,1,0:T(8,128)}, u32[]{:S(2)}, u32[]{:S(2)}) async-start(f32[128,1,1,1,128,128]{5,4,3,2,1,0:T(8,128)} %bitcast.96), calls=%async_computation.1 | async-start | bytes 16777216 | tf_op jit(solution)/shard_map/all_to_all | solution.py:87
  126.1 0.3 all-gather.5.cloned.1.call-start
  127.7 97.5 %all-to-all-done.1 = f32[128,1,1,1,128,128]{5,4,3,2,1,0:T(8,128)} async-done(((f32[128,1,1,1,128,128]{5,4,3,2,1,0:T(8,128)}), f32[128,1,1,1,128,128]{5,4,3,2,1,0:T(8,128)}, u32[]{:S(2)}, u32[]{:S(2)}) %all-to-all-start.1) | async-done | bytes 8388640 | tf_op jit(solution)/shard_map/all_to_all | solution.py:87
  225.3 7.2 %fusion = f32[128,128,128]{2,1,0:T(8,128)} fusion(f32[128,1,1,1,128,128]{5,4,3,2,1,0:T(8,128)} %all-to-all-done.1, pred[128]{0:T(512)(128)(4,1)S(1)} %and_bitcast_fusion), kind=kLoop, calls=%fused_computation.5 | loop fusion | flops 2097152 | bytes 16777344 | tf_op jit(solution)/shard_map/jit(_where)/select_n | solution.py:89
  232.5 0.1 broadcast_in_dim.103
  232.6 19.2 %scatter_fusion.1 = f32[6,3,128,128]{3,2,1,0:T(8,128)S(1)} fusion(f32[6,3,128,128]{3,2,1,0:T(8,128)S(1)} %broadcast_in_dim.103, s32[128]{0:T(128)S(1)} %get-tuple-element.27, f32[128,128,128]{2,1,0:T(8,128)} %fusion), kind=kCustom, calls=%fused_computation.3 | custom fusion | flops 2097152 | bytes 25166848 | tf_op jit(solution)/shard_map/scatter-add | solution.py:95
  251.8 0.0 copy-start.1
  251.8 0.8 copy.34
  252.6 0.4 copy-done.1
  253.1 1.1 fusion.27
  254.1 0.0 copy-start.2
  254.2 0.0 all-gather.5.cloned.1.call-update
  254.2 0.0 all-gather.3.cloned.1.call-start
  254.2 0.7 all-gather.3.cloned.1.call-update
  255.6 0.6 compare_select_fusion
  256.2 35.2 %all-gather.5.cloned.1.call-done = bf16[6144,384]{1,0:T(8,128)(2,1)} async-done(((bf16[768,384]{1,0:T(8,128)(2,1)}), bf16[6144,384]{1,0:T(8,128)(2,1)}) %all-gather.5.cloned.1.call-update) | async-done | bytes 4718608 | tf_op jit(solution)/shard_map/all_gather | solution.py:103
  291.4 86.1 %all-gather.3.cloned.1.call-done = bf16[768,6144]{1,0:T(8,128)(2,1)} async-done(((bf16[768,384]{1,0:T(8,128)(2,1)}), bf16[768,6144]{1,0:T(8,128)(2,1)}) %all-gather.3.cloned.1.call-update) | async-done | bytes 9437200 | tf_op jit(solution)/shard_map/all_gather | solution.py:105
  377.5 9.9 %subtract_select_fusion = f32[768,384]{1,0:T(8,128)} fusion(pred[]{:T(512)} %bitcast.30, f32[768,384]{1,0:T(8,128)S(1)} %copy-done.1, f32[768,384]{1,0:T(8,128)S(1)} %get-tuple-element.26, f32[]{:T(128)} %bitcast.94, f32[]{:T(128)} %bitcast.92, s32[384]{0:T(512)S(1)} %iota_add_fusion.1, s32[768]{0:T(1024)S(1)} %iota_add_fusion, ...), kind=kOutput, calls=%fused_computation.19 | convolution fusion | flops 3626237952 | bytes 17699336 | tf_op jit(solution)/shard_map/dot_general | solution.py:104
  387.3 0.0 copy-done.2
  (11 shorter events, 0.1 us)
Async XLA Ops:
  18.6 11.9 %copy-start.3 = (s32[128,8]{0,1:T(8,128)S(1)}, s32[128,8]{0,1:T(8,128)}, u32[]{:S(2)}) copy-start(s32[128,8]{0,1:T(8,128)} %param.14) | copy-start | bytes 12292
  18.6 62.9 %all-to-all-start = ((bf16[128,1,1,1,128,128]{5,4,3,2,1,0:T(8,128)(2,1)}), bf16[128,1,1,1,128,128]{5,4,3,2,1,0:T(8,128)(2,1)}, u32[]{:S(2)}, u32[]{:S(2)}) async-start(bf16[128,1,1,1,128,128]{5,4,3,2,1,0:T(8,128)(2,1)} %fusion.2), calls=%async_computation | async-start | bytes 8388608 | tf_op jit(solution)/shard_map/all_to_all | solution.py:56
  31.0 5.5 %copy-start.4 = (f32[1,1536]{1,0:T(1,128)S(1)}, f32[1,1536]{1,0:T(1,128)}, u32[]{:S(2)}) copy-start(f32[1,1536]{1,0:T(1,128)} %param.12) | copy-start | bytes 18436
  84.6 1.9 copy-start
  120.2 105.1 %all-to-all-start.1 = ((f32[128,1,1,1,128,128]{5,4,3,2,1,0:T(8,128)}), f32[128,1,1,1,128,128]{5,4,3,2,1,0:T(8,128)}, u32[]{:S(2)}, u32[]{:S(2)}) async-start(f32[128,1,1,1,128,128]{5,4,3,2,1,0:T(8,128)} %bitcast.96), calls=%async_computation.1 | async-start | bytes 16777216 | tf_op jit(solution)/shard_map/all_to_all | solution.py:87
  126.1 165.3 %all-gather.5.cloned.1.call-start = ((), (), s32[]{:S(2)}) async-start(), calls=%async_computation.3 | async-start | bytes 5308416 | tf_op jit(solution)/shard_map/all_gather | solution.py:103
  251.8 1.3 copy-start.1
  254.1 133.2 %copy-start.2 = (f32[768,384]{1,0:T(8,128)}, f32[768,384]{1,0:T(8,128)S(1)}, u32[]{:S(2)}) copy-start(f32[768,384]{1,0:T(8,128)S(1)} %get-tuple-element.26) | copy-start | bytes 3538948
  254.2 123.3 %all-gather.3.cloned.1.call-start = ((), (), s32[]{:S(2)}) async-start(), calls=%async_computation.2 | async-start | bytes 10027008 | tf_op jit(solution)/shard_map/all_gather | solution.py:105
Sparse Core Ops, SparseCore 0:
  254.3 37.0 all-gather.4
  294.1 83.3 all-gather.2
where the time goes:
time: 395 us; the launch traced here: 394 us
  waiting for transfers between devices  265 us (67%)
  local copies, waits for them, and re-layouts  41.2 us (10%)
  other arithmetic  34.6 us (9%)
  matrix products  18.8 us (5%)
  starting transfers between devices  18.1 us (5%)
  between operations  16.9 us (4%)
    all_to_all x1, waiting for transfers between devices, body(): lax.all_to_all(returning, ('row', 'col'), split_axis=0, concat_axis=0, ti...  97.5 us
    all_gather x1, waiting for transfers between devices, body(): lax.all_gather(rounded, 'col', axis=1, tiled=True)  86.1 us
    all_to_all x1, waiting for transfers between devices, body(): lax.all_to_all(outgoing, ('row', 'col'), split_axis=0, concat_axis=0, til...  45 us
    all_gather x1, waiting for transfers between devices, body(): column_block = lax.all_gather(rounded, 'row', axis=0, tiled=True)  35.2 us
    scatter-add x1, other arithmetic, body(): summed = jnp.zeros((band_rows, band_cols, TILE, TILE), jnp.float32).at[ro...  19.2 us
    scatter x1, local copies, waits for them, and re-layouts, body(): returning.at[source, batch_slot, slot_row[:, :, None], slot_col[:, None, :]]  12 us
    all_to_all x1, starting transfers between devices, body(): lax.all_to_all(outgoing, ('row', 'col'), split_axis=0, concat_axis=0, til...  11.9 us
    dot_general x1, matrix products, body(): jnp.dot(lax.all_gather(rounded, 'col', axis=1, tiled=True), column_block,...  9.85 us
  transfers between devices with their start and end apart: 4, of which 4 were waited for; matrix products, arithmetic and copies ran while one was open for 2% of the time, Pallas kernels for 0%

commit v1 on v0

--- a/solution.py
+++ b/solution.py
@@ -1,9 +1,215 @@
 import jax
 import jax.numpy as jnp
 from jax import lax
+from jax.experimental import pallas as pl
+from jax.experimental.pallas import tpu as pltpu
 from jax.sharding import PartitionSpec as P
 
+MESH = pl.DeviceIdType.MESH
 TILE = 128
+RING = 4
+
+
+def turn(value, step):
+    return lax.rem(value + (step % RING), RING)
+
+
+def square_kernel(
+    own_ref, start_ref, mix_ref, out_ref, rows_ref, cols_ref, row_send, row_recv, col_send, col_recv, core_send, core_recv, own_sem
+):
+    row, col = lax.axis_index("row"), lax.axis_index("col")
+    z, core = row // 2, lax.rem(row, 2)
+    x, y = col // RING, lax.rem(col, RING)
+    tall, wide = own_ref.shape
+    half = tall // 2
+    quarter = half // 2
+
+    def device(axis, step):
+        if axis == "x":
+            return (row, turn(x, step) * RING + y)
+        if axis == "y":
+            return (row, x * RING + turn(y, step))
+        if axis == "z":
+            return (turn(z, step) * 2 + core, col)
+        return (z * 2 + 1 - core, col)
+
+    def hop(place):
+        position, part = place
+        if position == 3:
+            return 1, 0
+        if position == 1:
+            return -1, 0
+        return (1, 3) if part == 0 else (-1, 1)
+
+    def row_block(side, dx, dy):
+        if dx == 0 and dy == 0:
+            return own_ref.at[pl.ds(side * half, half)]
+        return rows_ref.at[side, dx, dy]
+
+    def row_copy(side, dx, dy, part=0):
+        first, second = (dx, dy) if side == 0 else (dy, dx)
+        axes = ("x", "y") if side == 0 else ("y", "x")
+        place = second if second else first
+        axis = axes[1] if second else axes[0]
+        step, source = hop((place, part))
+        origin = (first, source) if second else (source, 0)
+        sx, sy = origin if side == 0 else origin[::-1]
+        src, dst = row_block(side, sx, sy), rows_ref.at[side, dx, dy]
+        if place == 2:
+            cut = pl.ds(part * quarter, quarter)
+            src, dst = src.at[cut], dst.at[cut]
+        return pltpu.make_async_remote_copy(
+            src_ref=src,
+            dst_ref=dst,
+            send_sem=row_send.at[side, dx, dy, part],
+            recv_sem=row_recv.at[side, dx, dy, part],
+            device_id=device(axis, step),
+            device_id_type=MESH,
+        )
+
+    def col_copy(dz, part=0):
+        step, source = hop((dz, part))
+        slot = turn(z, source)
+        src = own_ref if source == 0 else cols_ref.at[slot, core]
+        dst = cols_ref.at[slot, core]
+        if dz == 2:
+            cut = pl.ds(part * half, half)
+            src, dst = src.at[cut], dst.at[cut]
+        return pltpu.make_async_remote_copy(
+            src_ref=src,
+            dst_ref=dst,
+            send_sem=col_send.at[dz, part],
+            recv_sem=col_recv.at[dz, part],
+            device_id=device("z", step),
+            device_id_type=MESH,
+        )
+
+    def core_copy(dz):
+        slot = turn(z, dz)
+        return pltpu.make_async_remote_copy(
+            src_ref=own_ref if dz == 0 else cols_ref.at[slot, core],
+            dst_ref=cols_ref.at[slot, core],
+            send_sem=core_send.at[dz],
+            recv_sem=core_recv.at[dz],
+            device_id=device("core", 1),
+            device_id_type=MESH,
+        )
+
+    def row_pair(side, first, second):
+        return (first, second) if side == 0 else (second, first)
+
+    barrier = pltpu.get_barrier_semaphore()
+    partners = [device(a, s) for a in ("x", "y", "z") for s in (1, -1)] + [device("core", 1)]
+    for partner in partners:
+        pl.semaphore_signal(barrier, inc=1, device_id=partner, device_id_type=MESH)
+    pl.semaphore_wait(barrier, len(partners))
+
+    started = []
+
+    def go(copy):
+        copy.start()
+        started.append(copy)
+
+    for place in (3, 1):
+        for side in (0, 1):
+            go(row_copy(side, *row_pair(side, place, 0)))
+    for place in (3, 1):
+        go(col_copy(place))
+    go(core_copy(0))
+    for place in (3, 1):
+        for side in (0, 1):
+            go(row_copy(side, *row_pair(side, 0, place)))
+    mine = pltpu.make_async_copy(own_ref, cols_ref.at[z, core], own_sem)
+    mine.start()
+
+    for place, part in ((3, 0), (1, 1)):
+        for side in (0, 1):
+            row_copy(side, *row_pair(side, place, 0)).wait_recv()
+            go(row_copy(side, *row_pair(side, 2, 0), part))
+        for side in (0, 1):
+            for second in (3, 1):
+                go(row_copy(side, *row_pair(side, place, second)))
+        col_copy(place).wait_recv()
+        go(col_copy(2, part))
+        go(core_copy(place))
+    for side in (0, 1):
+        for part in (0, 1):
+            row_copy(side, *row_pair(side, 2, 0), part).wait_recv()
+        for second in (3, 1):
+            go(row_copy(side, *row_pair(side, 2, second)))
+    for part in (0, 1):
+        col_copy(2, part).wait_recv()
+    go(core_copy(2))
+
+    def second_ring(first):
+        for place, part in ((3, 0), (1, 1)):
+            for side in (0, 1):
+                row_copy(side, *row_pair(side, first, place)).wait_recv()
+                go(row_copy(side, *row_pair(side, first, 2), part))
+
+    def multiply(side, dx, dy):
+        index = turn(x, dx) * RING + turn(y, dy)
+        owner, cut = index // 2, lax.rem(index, 2)
+        factor = cols_ref[owner // 2, lax.rem(owner, 2), pl.ds(pl.multiple_of(cut * wide, wide), wide), :]
+        product = jnp.dot(row_block(side, dx, dy)[...], factor, preferred_element_type=jnp.float32)
+        spot = pl.ds(side * half, half)
+        if dx == 0 and dy == 0:
+            out_ref[spot, :] = product
+        else:
+            out_ref[spot, :] += product
+
+    second_ring(0)
+    mine.wait()
+    for dz in range(RING):
+        core_copy(dz).wait_recv()
+    for side in (0, 1):
+        for first in range(RING):
+            multiply(side, *row_pair(side, first, 0))
+        for place in (3, 1):
+            multiply(side, *row_pair(side, 0, place))
+    for first in (3, 1, 2):
+        second_ring(first)
+        for side in (0, 1):
+            for place in (3, 1):
+                multiply(side, *row_pair(side, first, place))
+    for first in (0, 3, 1, 2):
+        for side in (0, 1):
+            for part in (0, 1):
+                row_copy(side, *row_pair(side, first, 2), part).wait_recv()
+            multiply(side, *row_pair(side, first, 2))
+    out_ref[...] = mix_ref[0] * out_ref[...] + mix_ref[1] * start_ref[...]
+    for copy in started:
+        copy.wait_send()
+
+
+def squared(rounded, start, mix):
+    tall, wide = rounded.shape
+    vmem = pl.BlockSpec(memory_space=pltpu.VMEM)
+    dma = pltpu.SemaphoreType.DMA
+    return pl.pallas_call(
+        square_kernel,
+        name="square_kernel",
+        out_shape=jax.ShapeDtypeStruct((tall, wide), jnp.float32),
+        in_specs=[vmem, vmem, pl.BlockSpec(memory_space=pltpu.SMEM)],
+        out_specs=vmem,
+        scratch_shapes=[
+            pltpu.VMEM((2, RING, RING, tall // 2, wide), jnp.bfloat16),
+            pltpu.VMEM((RING, 2, tall, wide), jnp.bfloat16),
+            dma((2, RING, RING, 2)),
+            dma((2, RING, RING, 2)),
+            dma((RING, 2)),
+            dma((RING, 2)),
+            dma((RING,)),
+            dma((RING,)),
+            dma,
+        ],
+        compiler_params=pltpu.CompilerParams(
+            collective_id=4, has_side_effects=True, vmem_limit_bytes=48 * 2**20
+        ),
+        cost_estimate=pl.CostEstimate(
+            flops=2 * tall * wide * tall * 8, bytes_accessed=4 * tall * wide * 4, transcendentals=0
+        ),
+    )(rounded, start, mix)
 
 
 SLATER = (3.0 / 3.141592653589793) ** (1.0 / 3.0)
@@ -100,13 +306,9 @@
     identity = (global_rows[:, None] == global_cols[None, :]).astype(jnp.float32)
     start = map_shift[0] * identity + map_scale[0] * (core_matrix + potential)
     rounded = start.astype(jnp.bfloat16)
-    column_block = lax.all_gather(rounded, "row", axis=0, tiled=True)
-    square = jnp.dot(
-        lax.all_gather(rounded, "col", axis=1, tiled=True),
-        column_block,
-        preferred_element_type=jnp.float32,
-    )
-    purified = jnp.where(branch_flags[0] == 0, square, 2.0 * start - square)
+    keep = branch_flags[0] == 0
+    mix = jnp.stack([jnp.where(keep, 1.0, -1.0), jnp.where(keep, 0.0, 2.0)]).astype(jnp.float32)
+    purified = squared(rounded, start, mix)
     return (jnp.stack(densities), potential, purified)
 
 

time: 395 us -> 308 us (0.78)
  waiting for transfers between devices: 265 us -> 142 us
  Pallas kernels: 0 us -> 57.1 us
  between operations: 16.9 us -> 3.47 us
  matrix products: 18.8 us -> 8.99 us
    all_gather x2 -> x0, waiting for transfers between devices: 121 us -> none  [the longest x1 86.1 us: body(): lax.all_gather(rounded, 'col', axis=1, tiled=True)]
    pallas_call x0 -> x1, Pallas kernels: none -> 57.1 us  [squared(): pl.pallas_call(square_kernel, name='square_kernel', out_shape=jax.ShapeDt...]
    dot_general x1 -> x0, matrix products: 9.85 us -> none  [body(): jnp.dot(lax.all_gather(rounded, 'col', axis=1, tiled=True), column_block,...]
    another operation x2 -> x1, local copies, waits for them, and re-layouts: 5.39 us -> 0.01 us  [the longest x1 5.39 us: body(): block_tiles = jnp.stack(contributions).reshape(per_device, blocks, TILE,...]
    transpose x0 -> x1, local copies, waits for them, and re-layouts: none -> 5.39 us  [body(): block_tiles = jnp.stack(contributions).reshape(per_device, blocks, TILE,...]
    unnamed x13 -> x12, local copies, waits for them, and re-layouts: 9.47 us -> 10.5 us
  transfers between devices with their start and end apart: 4 -> 2, of which waited for: 4 -> 2; matrix products, arithmetic and copies ran while one was open for 2% -> 2% of each run, Pallas kernels for 0% -> 0%
where the time goes in v1:
time: 308 us; the launch traced here: 306 us
  waiting for transfers between devices  142 us (46%)
  Pallas kernels  57.1 us (19%)
  local copies, waits for them, and re-layouts  42.1 us (14%)
  other arithmetic  34.8 us (11%)
  starting transfers between devices  17.8 us (6%)
  matrix products  8.99 us (3%)
  between operations  3.47 us (1%)
    all_to_all x1, waiting for transfers between devices, body(): lax.all_to_all(returning, ('row', 'col'), split_axis=0, concat_axis=0, ti...  96.4 us
    pallas_call x1, Pallas kernels, squared(): pl.pallas_call(square_kernel, name='square_kernel', out_shape=jax.ShapeDt...  57.1 us
    all_to_all x1, waiting for transfers between devices, body(): lax.all_to_all(outgoing, ('row', 'col'), split_axis=0, concat_axis=0, til...  45.2 us
    scatter-add x1, other arithmetic, body(): summed = jnp.zeros((band_rows, band_cols, TILE, TILE), jnp.float32).at[ro...  19.2 us
    scatter x1, local copies, waits for them, and re-layouts, body(): returning.at[source, batch_slot, slot_row[:, :, None], slot_col[:, None, :]]  11.9 us
    all_to_all x1, starting transfers between devices, body(): lax.all_to_all(outgoing, ('row', 'col'), split_axis=0, concat_axis=0, til...  11.7 us
    unnamed x12, local copies, waits for them, and re-layouts  10.5 us
    select_n x1, other arithmetic, body(): landed = jnp.where(owned[:, :, :, None, None], landed, jnp.float32(0.0))  7.22 us
  transfers between devices with their start and end apart: 2, of which 2 were waited for; matrix products, arithmetic and copies ran while one was open for 2% of the time, Pallas kernels for 0%

profile of v1, /device:TPU:0, one launch (start us, length us, event | category | flops | bytes accessed | tf_op | source)
XLA Modules:
  0.0 305.8 jit_solution(12278630140443091142)
XLA Ops:
  0.7 0.8 compare_select_fusion.5
  1.5 0.8 and_bitcast_fusion
  2.3 2.0 reshape.431
  4.3 0.1 copy.47
  4.4 3.1 %gather_fusion = bf16[128,128,128]{2,1,0:T(8,128)(2,1)} fusion(bf16[6,3,128,128]{3,2,1,0:T(8,128)(2,1)S(1)} %bitcast.92, s32[128]{0:T(128)S(1)} %bitcast.95), kind=kCustom, calls=%fused_computation | custom fusion | bytes 8389632 | tf_op jit(solution)/shard_map/gather | solution.py:259
  7.5 4.5 %fusion.2 = bf16[128,1,1,1,128,128]{5,4,3,2,1,0:T(8,128)(2,1)} fusion(bf16[128,128,128]{2,1,0:T(8,128)(2,1)} %gather_fusion, pred[128]{0:T(512)(128)(4,1)S(1)} %and_bitcast_fusion), kind=kLoop, calls=%fused_computation.10 | loop fusion | flops 2097152 | bytes 8388736 | tf_op jit(solution)/shard_map/jit(_where)/select_n | solution.py:260
  12.0 0.0 copy-start.2
  12.1 11.7 %all-to-all-start = ((bf16[128,1,1,1,128,128]{5,4,3,2,1,0:T(8,128)(2,1)}), bf16[128,1,1,1,128,128]{5,4,3,2,1,0:T(8,128)(2,1)}, u32[]{:S(2)}, u32[]{:S(2)}) async-start(bf16[128,1,1,1,128,128]{5,4,3,2,1,0:T(8,128)(2,1)} %fusion.2), calls=%async_computation | async-start | bytes 8388608 | tf_op jit(solution)/shard_map/all_to_all | solution.py:262
  23.7 0.0 copy-done.2
  23.8 0.2 multiply_reduce_fusion
  24.0 0.1 compare_select_fusion.1
  24.1 0.1 broadcast_in_dim.61
  24.2 0.1 reshape.399
  24.3 0.0 copy-start.3
  24.3 4.7 %copy.27 = bf16[1,1536,1024]{1,2,0:T(8,128)(2,1)} copy(bf16[1,1536,1024]{2,1,0:T(8,128)(2,1)} %param.11) | data formatting | bytes 6291456 | tf_op args[0]
  29.6 0.1 reshape.411
  29.7 0.0 copy-done.3
  29.7 45.2 %all-to-all-done = bf16[128,1,1,1,128,128]{5,4,3,2,1,0:T(8,128)(2,1)} async-done(((bf16[128,1,1,1,128,128]{5,4,3,2,1,0:T(8,128)(2,1)}), bf16[128,1,1,1,128,128]{5,4,3,2,1,0:T(8,128)(2,1)}, u32[]{:S(2)}, u32[]{:S(2)}) %all-to-all-start) | async-done | bytes 4194336 | tf_op jit(solution)/shard_map/all_to_all | solution.py:262
  74.9 3.1 %gather_fusion.1 = bf16[64,128,128]{2,1,0:T(8,128)(2,1)S(1)} fusion(bf16[128,1,1,1,128,128]{5,4,3,2,1,0:T(8,128)(2,1)} %all-to-all-done, s32[64]{0:T(128)S(1)} %reshape.399), kind=kCustom, calls=%fused_computation.1 | custom fusion | bytes 4195328 | tf_op jit(solution)/shard_map/gather | solution.py:272
  78.1 0.0 copy-start
  78.1 1.4 copy.26
  79.5 0.5 copy-done
  80.0 5.3 %fusion.1 = f32[1536]{0:T(1024)S(1)} fusion(bf16[1,1536,1024]{2,1,0:T(8,128)(2,1)S(1)} %copy-done, bf16[1,1536,1024]{1,2,0:T(8,128)(2,1)} %copy.27, bf16[128,8,8,128]{3,2,1,0:T(8,128)(2,1)S(1)} %bitcast.98), kind=kOutput, calls=%fused_computation.7 | convolution fusion | flops 3225942528 | bytes 8394752 | tf_op jit(solution)/shard_map/dot_general | solution.py:276
  85.3 3.7 %fusion.9 = f32[128,8,8,128]{3,1,2,0:T(8,128)S(1)} fusion(bf16[1,1536,1024]{2,1,0:T(8,128)(2,1)S(1)} %copy-done, f32[1536]{0:T(1024)S(1)} %multiply_select_fusion), kind=kOutput, calls=%fused_computation.16 | convolution fusion | flops 3225944064 | bytes 7346176 | tf_op jit(solution)/shard_map/dot_general | solution.py:282
  89.0 3.0 copy.38
  92.0 5.4 %copy.28 = f32[1,8,8,128,128]{4,3,2,1,0:T(8,128)} copy(f32[1,8,8,128,128]{3,1,4,2,0:T(8,128)} %bitcast.94) | data formatting | bytes 8388608 | tf_op jit(solution)/shard_map/transpose | solution.py:287
  97.4 4.3 %broadcast.385 = f32[128,128,128]{2,1,0:T(8,128)} broadcast(f32[]{:T(128)} %constant.100.clone.1), dimensions={} | broadcast | bytes 8388612 | tf_op jit(solution)/shard_map/broadcast_in_dim | solution.py:289
  101.6 11.9 %scatter_fusion = f32[128,128,128]{2,1,0:T(8,128)} fusion(f32[128,128,128]{2,1,0:T(8,128)} %broadcast.385, s32[64]{0:T(128)S(1)} %reshape.411, f32[64,128,128]{2,1,0:T(8,128)} %bitcast.93), kind=kCustom, calls=%fused_computation.2 | custom fusion | bytes 12583168 | tf_op jit(solution)/shard_map/scatter | solution.py:290
  113.5 6.1 %all-to-all-start.1 = ((f32[128,1,1,1,128,128]{5,4,3,2,1,0:T(8,128)}), f32[128,1,1,1,128,128]{5,4,3,2,1,0:T(8,128)}, u32[]{:S(2)}, u32[]{:S(2)}) async-start(f32[128,1,1,1,128,128]{5,4,3,2,1,0:T(8,128)} %bitcast.91), calls=%async_computation.1 | async-start | bytes 16777216 | tf_op jit(solution)/shard_map/all_to_all | solution.py:293
  121.6 0.1 pad_maximum_fusion.mix_ref
  121.7 0.6 compare_select_fusion
  122.3 96.4 %all-to-all-done.1 = f32[128,1,1,1,128,128]{5,4,3,2,1,0:T(8,128)} async-done(((f32[128,1,1,1,128,128]{5,4,3,2,1,0:T(8,128)}), f32[128,1,1,1,128,128]{5,4,3,2,1,0:T(8,128)}, u32[]{:S(2)}, u32[]{:S(2)}) %all-to-all-start.1) | async-done | bytes 8388640 | tf_op jit(solution)/shard_map/all_to_all | solution.py:293
  218.6 7.2 %fusion = f32[128,128,128]{2,1,0:T(8,128)} fusion(f32[128,1,1,1,128,128]{5,4,3,2,1,0:T(8,128)} %all-to-all-done.1, pred[128]{0:T(512)(128)(4,1)S(1)} %and_bitcast_fusion), kind=kLoop, calls=%fused_computation.5 | loop fusion | flops 2097152 | bytes 16777344 | tf_op jit(solution)/shard_map/jit(_where)/select_n | solution.py:295
  225.9 0.1 broadcast_in_dim.103
  226.0 19.2 %scatter_fusion.1 = f32[6,3,128,128]{3,2,1,0:T(8,128)S(1)} fusion(f32[6,3,128,128]{3,2,1,0:T(8,128)S(1)} %broadcast_in_dim.103, s32[128]{0:T(128)S(1)} %get-tuple-element.28, f32[128,128,128]{2,1,0:T(8,128)} %fusion), kind=kCustom, calls=%fused_computation.3 | custom fusion | flops 2097152 | bytes 25166848 | tf_op jit(solution)/shard_map/scatter-add | solution.py:301
  245.2 0.0 copy-start.1
  245.2 0.8 copy.35
  246.0 0.4 copy-done.1
  246.4 1.2 fusion.27
  247.7 57.1 %square_kernel.1 = f32[768,384]{1,0:T(8,128)S(1)} custom-call(bf16[768,384]{1,0:T(8,128)(2,1)S(1)} %get-tuple-element.25.own_ref, f32[768,384]{1,0:T(8,128)S(1)} %get-tuple-element.26.start_ref, f32[2]{0:T(128)S(1)} %pad_maximum_fusion.mix_ref), custom_call_target="tpu_custom_call" | custom-call | flops 3623878656 | bytes 4718592 | tf_op jit(solution)/shard_map/square_kernel/pallas_call | solution.py:189
  304.8 1.0 copy.55
  (11 shorter events, 0.1 us)
Async XLA Ops:
  12.0 11.7 %copy-start.2 = (s32[128,8]{0,1:T(8,128)S(1)}, s32[128,8]{0,1:T(8,128)}, u32[]{:S(2)}) copy-start(s32[128,8]{0,1:T(8,128)} %param.14) | copy-start | bytes 12292
  12.1 62.9 %all-to-all-start = ((bf16[128,1,1,1,128,128]{5,4,3,2,1,0:T(8,128)(2,1)}), bf16[128,1,1,1,128,128]{5,4,3,2,1,0:T(8,128)(2,1)}, u32[]{:S(2)}, u32[]{:S(2)}) async-start(bf16[128,1,1,1,128,128]{5,4,3,2,1,0:T(8,128)(2,1)} %fusion.2), calls=%async_computation | async-start | bytes 8388608 | tf_op jit(solution)/shard_map/all_to_all | solution.py:262
  24.3 5.5 %copy-start.3 = (f32[1,1536]{1,0:T(1,128)S(1)}, f32[1,1536]{1,0:T(1,128)}, u32[]{:S(2)}) copy-start(f32[1,1536]{1,0:T(1,128)} %param.12) | copy-start | bytes 18436
  78.1 1.9 copy-start
  113.5 105.1 %all-to-all-start.1 = ((f32[128,1,1,1,128,128]{5,4,3,2,1,0:T(8,128)}), f32[128,1,1,1,128,128]{5,4,3,2,1,0:T(8,128)}, u32[]{:S(2)}, u32[]{:S(2)}) async-start(f32[128,1,1,1,128,128]{5,4,3,2,1,0:T(8,128)} %bitcast.91), calls=%async_computation.1 | async-start | bytes 16777216 | tf_op jit(solution)/shard_map/all_to_all | solution.py:293
  245.2 1.3 copy-start.1

commit v2 on v1

--- a/solution.py
+++ b/solution.py
@@ -7,7 +7,13 @@
 
 MESH = pl.DeviceIdType.MESH
 TILE = 128
+PART = TILE // 2
+BLK = 8
+BS = 6
 RING = 4
+COLS = 16
+DEVICES = 128
+STRIDE = 37
 
 
 def turn(value, step):
@@ -212,6 +218,242 @@
     )(rounded, start, mix)
 
 
+def device_at(index):
+    return index // COLS, lax.rem(index, COLS)
+
+
+def offset_device(row, col, step):
+    z, core = row // 2, lax.rem(row, 2)
+    x, y = col // RING, lax.rem(col, RING)
+    dx, dy = step // 32, lax.rem(step // 8, RING)
+    dz, dcore = lax.rem(step // 2, RING), lax.rem(step, 2)
+    there = lax.rem(z + dz, RING) * 2 + lax.rem(core + dcore, 2)
+    return there, lax.rem(x + dx, RING) * RING + lax.rem(y + dy, RING)
+
+
+def spread(step):
+    return lax.rem(step * STRIDE, DEVICES)
+
+
+def greet_all(row, col):
+    barrier = pltpu.get_barrier_semaphore()
+
+    @pl.loop(1, DEVICES)
+    def _(step):
+        pl.semaphore_signal(barrier, inc=1, device_id=offset_device(row, col, step), device_id_type=MESH)
+
+    pl.semaphore_wait(barrier, DEVICES - 1)
+
+
+def tiles_in_kernel(
+    tiles_ref, dens_ref, sub_ref, both_ref, out_ref, pair_send, pair_recv, own_sem, send_sem, recv_sem
+):
+    row, col = lax.axis_index("row"), lax.axis_index("col")
+    slot, side = col // 2, lax.rem(col, 2)
+    other = 1 - side
+    greet_all(row, col)
+    partner = (row, slot * 2 + other)
+    pairs, mines = [], []
+    for tile in range(BS // 2):
+        cut = pl.ds(tile * TILE, TILE)
+        spot = both_ref.at[pl.ds((side * (BS // 2) + tile) * BS, BS)]
+        pairs.append(
+            pltpu.make_async_remote_copy(
+                src_ref=dens_ref.at[:, pl.ds(pl.multiple_of(other * PART, PART), PART), cut],
+                dst_ref=spot,
+                send_sem=pair_send.at[tile],
+                recv_sem=pair_recv.at[tile],
+                device_id=partner,
+                device_id_type=MESH,
+            )
+        )
+        mines.append(
+            pltpu.make_async_copy(
+                dens_ref.at[:, pl.ds(pl.multiple_of(side * PART, PART), PART), cut], spot, own_sem.at[tile]
+            )
+        )
+    for copy in pairs + mines:
+        copy.start()
+    for copy in mines + pairs:
+        copy.wait()
+    spot_rows = pl.ds(pl.multiple_of(row * TILE + side * PART, PART), PART)
+    spot_cols = pl.ds(pl.multiple_of(slot * TILE, TILE), TILE)
+
+    def stage(target):
+        batch = target[0] * COLS + target[1]
+        tile_row = tiles_ref[batch * BLK + row] - row * BS
+        tile_col = tiles_ref[batch * BLK + slot] - slot * BS
+        out_ref[batch] = both_ref[jnp.clip(tile_col * BS + tile_row, 0, BS * BS - 1)]
+        return batch
+
+    @pl.loop(1, DEVICES)
+    def _(count):
+        target = offset_device(row, col, spread(count))
+        batch = stage(target)
+        pltpu.make_async_remote_copy(
+            src_ref=out_ref.at[batch],
+            dst_ref=sub_ref.at[spot_rows, spot_cols],
+            send_sem=send_sem,
+            recv_sem=recv_sem,
+            device_id=target,
+            device_id_type=MESH,
+        ).start()
+
+    batch = stage((row, col))
+    pltpu.make_async_copy(out_ref.at[batch], sub_ref.at[spot_rows, spot_cols], recv_sem).start()
+    pltpu.make_async_copy(sub_ref, sub_ref, recv_sem).wait()
+    rest = out_ref.at[pl.ds(0, DEVICES - 1)]
+    pltpu.make_async_copy(rest, rest, send_sem).wait()
+
+
+def tiles_in(tiles, density):
+    dma = pltpu.SemaphoreType.DMA
+    tall, wide = density.shape
+    return pl.pallas_call(
+        tiles_in_kernel,
+        name="tiles_in_kernel",
+        out_shape=jax.ShapeDtypeStruct((BLK * TILE, BLK * TILE), jnp.bfloat16),
+        in_specs=[pl.BlockSpec(memory_space=pltpu.SMEM), pl.BlockSpec(memory_space=pltpu.VMEM)],
+        out_specs=pl.BlockSpec(memory_space=pltpu.VMEM),
+        scratch_shapes=[
+            pltpu.VMEM((BS * BS, PART, TILE), jnp.bfloat16),
+            pltpu.VMEM((DEVICES, PART, TILE), jnp.bfloat16),
+            dma((BS // 2,)),
+            dma((BS // 2,)),
+            dma((BS // 2,)),
+            dma,
+            dma,
+        ],
+        compiler_params=pltpu.CompilerParams(
+            collective_id=1, has_side_effects=True, vmem_limit_bytes=32 * 2**20
+        ),
+        cost_estimate=pl.CostEstimate(flops=0, bytes_accessed=8 * 2**20, transcendentals=0),
+    )(tiles.reshape(-1), density.reshape(BS, TILE, wide))
+
+
+def tiles_back_kernel(
+    block_ref,
+    prev_ref,
+    last_ref,
+    map_ref,
+    core_ref,
+    xc_ref,
+    start_ref,
+    rounded_ref,
+    landed_ref,
+    sums_ref,
+    give_ref,
+    got_ref,
+    pair_send,
+    pair_recv,
+    send_sem,
+    recv_sem,
+):
+    row, col = lax.axis_index("row"), lax.axis_index("col")
+    slot, side = col // 2, lax.rem(col, 2)
+    other = 1 - side
+    me = row * COLS + col
+    greet_all(row, col)
+
+    def piece(target):
+        there_row, there_col = target
+        first = there_row * TILE + lax.rem(there_col, 2) * PART
+        return block_ref.at[
+            pl.ds(pl.multiple_of(first, PART), PART),
+            pl.ds(pl.multiple_of(there_col // 2 * TILE, TILE), TILE),
+        ]
+
+    @pl.loop(1, DEVICES)
+    def _(count):
+        target = offset_device(row, col, spread(count))
+        pltpu.make_async_remote_copy(
+            src_ref=piece(target),
+            dst_ref=landed_ref.at[me],
+            send_sem=send_sem,
+            recv_sem=recv_sem,
+            device_id=target,
+            device_id_type=MESH,
+        ).start()
+
+    pltpu.make_async_copy(piece((row, col)), landed_ref.at[me], recv_sem).start()
+    sums_ref[DEVICES] = jnp.zeros((PART, TILE), jnp.float32)
+    pltpu.make_async_copy(landed_ref, landed_ref, recv_sem).wait()
+
+    @pl.loop(0, DEVICES)
+    def _(batch):
+        sums_ref[batch] = sums_ref[prev_ref[batch]] + landed_ref[batch].astype(jnp.float32)
+
+    def total(tile_row, half, tile):
+        return sums_ref[last_ref[tile_row * BS + half * (BS // 2) + tile]]
+
+    for tile_row in range(BS):
+        for tile in range(BS // 2):
+            cut = slice(tile * TILE, (tile + 1) * TILE)
+            give_ref[tile_row, :, cut] = total(tile_row, other, tile).astype(give_ref.dtype)
+    pair = pltpu.make_async_remote_copy(
+        src_ref=give_ref,
+        dst_ref=got_ref,
+        send_sem=pair_send,
+        recv_sem=pair_recv,
+        device_id=(row, slot * 2 + other),
+        device_id_type=MESH,
+    )
+    pair.start()
+
+    wide = xc_ref.shape[1]
+
+    def finish(first, value):
+        spot = pl.ds(pl.multiple_of(first, PART), PART)
+        xc_ref[spot, :] = value
+        down = lax.broadcasted_iota(jnp.int32, value.shape, 0) + (row * BS * TILE + first)
+        across = lax.broadcasted_iota(jnp.int32, value.shape, 1) + col * wide
+        shift = jnp.where(down == across, map_ref[0], jnp.float32(0.0))
+        start = shift + map_ref[1] * (core_ref[spot, :] + value)
+        start_ref[spot, :] = start
+        rounded_ref[spot, :] = start.astype(jnp.bfloat16)
+
+    for tile_row in range(BS):
+        mine = jnp.concatenate([total(tile_row, side, tile) for tile in range(BS // 2)], axis=1)
+        finish(tile_row * TILE + side * PART, mine)
+    pair.wait()
+    for tile_row in range(BS):
+        finish(tile_row * TILE + other * PART, got_ref[tile_row].astype(jnp.float32))
+    rest = landed_ref.at[pl.ds(0, DEVICES - 1)]
+    pltpu.make_async_copy(rest, rest, send_sem).wait()
+
+
+def tiles_back(block, prev, last, mapping, core_matrix):
+    dma = pltpu.SemaphoreType.DMA
+    tall, wide = core_matrix.shape
+    vmem = pl.BlockSpec(memory_space=pltpu.VMEM)
+    smem = pl.BlockSpec(memory_space=pltpu.SMEM)
+    return pl.pallas_call(
+        tiles_back_kernel,
+        name="tiles_back_kernel",
+        out_shape=(
+            jax.ShapeDtypeStruct((tall, wide), jnp.float32),
+            jax.ShapeDtypeStruct((tall, wide), jnp.float32),
+            jax.ShapeDtypeStruct((tall, wide), jnp.bfloat16),
+        ),
+        in_specs=[vmem, smem, smem, smem, vmem],
+        out_specs=(vmem, vmem, vmem),
+        scratch_shapes=[
+            pltpu.VMEM((DEVICES, PART, TILE), jnp.bfloat16),
+            pltpu.VMEM((DEVICES + 1, PART, TILE), jnp.float32),
+            pltpu.VMEM((BS, PART, wide), jnp.bfloat16),
+            pltpu.VMEM((BS, PART, wide), jnp.bfloat16),
+            dma,
+            dma,
+            dma,
+            dma,
+        ],
+        compiler_params=pltpu.CompilerParams(
+            collective_id=2, has_side_effects=True, vmem_limit_bytes=40 * 2**20
+        ),
+        cost_estimate=pl.CostEstimate(flops=0, bytes_accessed=16 * 2**20, transcendentals=0),
+    )(block, prev, last, mapping, core_matrix)
+
+
 SLATER = (3.0 / 3.141592653589793) ** (1.0 / 3.0)
 
 
@@ -230,86 +472,36 @@
     map_scale,
     branch_flags,
 ):
-    row_count = lax.axis_size("row")
-    col_count = lax.axis_size("col")
-    devices_all = row_count * col_count
-    row_index = lax.axis_index("row")
-    col_index = lax.axis_index("col")
-    local_rows, local_cols = density.shape
-    band_rows = local_rows // TILE
-    band_cols = local_cols // TILE
-    per_device = basis_values.shape[0]
-    batch_total = basis_tiles.shape[0]
+    row, col = lax.axis_index("row"), lax.axis_index("col")
     points = basis_values.shape[1]
-    width = basis_values.shape[2]
-    blocks = width // TILE
-    block_span = band_rows * row_count // blocks
-    slots_row = max(1, band_rows // block_span)
-    slots_col = max(1, band_cols // block_span)
-    first_row = row_index * band_rows // block_span
-    first_col = col_index * band_cols // block_span
-    wanted_rows = jnp.take(basis_tiles, first_row + jnp.arange(slots_row, dtype=jnp.int32), axis=1)
-    wanted_cols = jnp.take(basis_tiles, first_col + jnp.arange(slots_col, dtype=jnp.int32), axis=1)
-    owned = (wanted_rows // band_rows == row_index)[:, :, None] & (
-        wanted_cols // band_cols == col_index
-    )[:, None, :]
-    local_row = jnp.clip(wanted_rows - row_index * band_rows, 0, band_rows - 1)
-    local_col = jnp.clip(wanted_cols - col_index * band_cols, 0, band_cols - 1)
-    tile_grid = density.reshape(band_rows, TILE, band_cols, TILE).transpose(0, 2, 1, 3)
-    outgoing = tile_grid[local_row[:, :, None], local_col[:, None, :]]
-    outgoing = jnp.where(owned[:, :, :, None, None], outgoing, jnp.zeros((), jnp.bfloat16))
-    outgoing = outgoing.reshape(devices_all, per_device, slots_row, slots_col, TILE, TILE)
-    arrived = lax.all_to_all(outgoing, ("row", "col"), split_axis=0, concat_axis=0, tiled=True)
-    my_start = (row_index * col_count + col_index) * per_device
-    my_tiles = lax.dynamic_slice_in_dim(basis_tiles, my_start, per_device, 0)
-    owner_row = my_tiles // band_rows
-    owner_col = my_tiles // band_cols
-    source = owner_row[:, :, None] * col_count + owner_col[:, None, :]
-    block_ids = jnp.arange(blocks, dtype=jnp.int32)[None, :]
-    slot_row = block_ids - owner_row * band_rows // block_span
-    slot_col = block_ids - owner_col * band_cols // block_span
-    batch_slot = jnp.arange(per_device, dtype=jnp.int32)[:, None, None]
-    gathered = arrived[source, batch_slot, slot_row[:, :, None], slot_col[:, None, :]]
-    submatrix = gathered.transpose(0, 1, 3, 2, 4).reshape(per_device, width, width)
+    submatrix = tiles_in(basis_tiles, density)
+
+    batches = jnp.arange(DEVICES, dtype=jnp.int32)
+    down = lax.dynamic_index_in_dim(basis_tiles, row, 1, keepdims=False) - row * BS
+    across = lax.dynamic_index_in_dim(basis_tiles, col // 2, 1, keepdims=False) - col // 2 * BS
+    key = down * BS + across
+    earlier = (key[:, None] == key[None, :]) & (batches[None, :] < batches[:, None])
+    prev = jnp.max(jnp.where(earlier, batches[None, :], -1), axis=1)
+    prev = jnp.where(prev < 0, DEVICES, prev)
+    hits = jnp.arange(BS * BS, dtype=jnp.int32)[:, None] == key[None, :]
+    last = jnp.max(jnp.where(hits, batches[None, :], -1), axis=1)
+    last = jnp.where(last < 0, DEVICES, last)
+
     point_ids = jnp.arange(points, dtype=jnp.int32)
     values = basis_values[0]
-    mixed = jnp.dot(values, submatrix[0], preferred_element_type=jnp.float32)
+    mixed = jnp.dot(values, submatrix, preferred_element_type=jnp.float32)
     local_density = jnp.sum(mixed * values.astype(jnp.float32), axis=1)
     live = point_ids < point_counts[0]
     local_density = jnp.where(live, local_density, jnp.float32(0.0))
     factor = jnp.where(live, quad_weights[0] * potential_factor(local_density), jnp.float32(0.0))
     weighted = (factor[:, None] * values).astype(jnp.bfloat16)
-    contributions = [jnp.dot(values.T, weighted, preferred_element_type=jnp.float32)]
-    densities = [local_density]
-    block_tiles = (
-        jnp.stack(contributions)
-        .reshape(per_device, blocks, TILE, blocks, TILE)
-        .transpose(0, 1, 3, 2, 4)
-    )
-    returning = jnp.zeros((devices_all, per_device, slots_row, slots_col, TILE, TILE), jnp.float32)
-    returning = returning.at[source, batch_slot, slot_row[:, :, None], slot_col[:, None, :]].set(
-        block_tiles
-    )
-    landed = lax.all_to_all(returning, ("row", "col"), split_axis=0, concat_axis=0, tiled=True)
-    landed = landed.reshape(batch_total, slots_row, slots_col, TILE, TILE)
-    landed = jnp.where(owned[:, :, :, None, None], landed, jnp.float32(0.0))
-    row_target = local_row[:, :, None]
-    col_target = local_col[:, None, :]
-    summed = (
-        jnp.zeros((band_rows, band_cols, TILE, TILE), jnp.float32)
-        .at[row_target, col_target]
-        .add(landed)
-    )
-    potential = summed.transpose(0, 2, 1, 3).reshape(local_rows, local_cols)
-    global_rows = row_index * local_rows + jnp.arange(local_rows, dtype=jnp.int32)
-    global_cols = col_index * local_cols + jnp.arange(local_cols, dtype=jnp.int32)
-    identity = (global_rows[:, None] == global_cols[None, :]).astype(jnp.float32)
-    start = map_shift[0] * identity + map_scale[0] * (core_matrix + potential)
-    rounded = start.astype(jnp.bfloat16)
+    block = jnp.dot(values.T, weighted, preferred_element_type=jnp.float32).astype(jnp.bfloat16)
+    mapping = jnp.concatenate([map_shift, map_scale])
+    potential, start, rounded = tiles_back(block, prev, last, mapping, core_matrix)
     keep = branch_flags[0] == 0
     mix = jnp.stack([jnp.where(keep, 1.0, -1.0), jnp.where(keep, 0.0, 2.0)]).astype(jnp.float32)
     purified = squared(rounded, start, mix)
-    return (jnp.stack(densities), potential, purified)
+    return (local_density[None], potential, purified)
 
 
 def solution(mesh):

time: 308 us -> 173 us (0.56)
  waiting for transfers between devices: 142 us -> 0 us
  Pallas kernels: 57.1 us -> 146 us
  local copies, waits for them, and re-layouts: 42.1 us -> 8.63 us
  other arithmetic: 34.8 us -> 1.87 us
  starting transfers between devices: 17.8 us -> 0 us
  matrix products: 8.99 us -> 12.7 us
    all_to_all x2 -> x0, waiting for transfers between devices: 142 us -> none  [the longest x1 96.4 us: body(): lax.all_to_all(returning, ('row', 'col'), split_axis=0, concat_axis=0, ti...]
    pallas_call x0 -> x2, Pallas kernels: none -> 92.6 us  [the longest x1 47.5 us: tiles_in(): pl.pallas_call(tiles_in_kernel, name='tiles_in_kernel', out_shape=jax.Sha...]
    scatter-add x1 -> x0, other arithmetic: 19.2 us -> none  [body(): summed = jnp.zeros((band_rows, band_cols, TILE, TILE), jnp.float32).at[ro...]
    all_to_all x2 -> x0, starting transfers between devices: 17.8 us -> none  [the longest x1 11.7 us: body(): lax.all_to_all(outgoing, ('row', 'col'), split_axis=0, concat_axis=0, til...]
    select_n x5 -> x2, other arithmetic: 12.6 us -> 0.01 us  [the longest x1 0.01 us: body(): last = jnp.where(last < 0, DEVICES, last)]
    scatter x1 -> x0, local copies, waits for them, and re-layouts: 11.9 us -> none  [body(): returning.at[source, batch_slot, slot_row[:, :, None], slot_col[:, None, :]]]
    gather x3 -> x0, local copies, waits for them, and re-layouts: 7.61 us -> none  [the longest x2 4.51 us: body(): arrived[source, batch_slot, slot_row[:, :, None], slot_col[:, None, :]]]
    transpose x1 -> x0, local copies, waits for them, and re-layouts: 5.39 us -> none  [body(): block_tiles = jnp.stack(contributions).reshape(per_device, blocks, TILE,...]
  transfers between devices with their start and end apart: 2 -> 0, of which waited for: 2 -> 0; matrix products, arithmetic and copies ran while one was open for 2% -> 0% of each run, Pallas kernels for 0% -> 0%
where the time goes in v2:
time: 173 us
  Pallas kernels  146 us (84%)
  matrix products  12.7 us (7%)
  local copies, waits for them, and re-layouts  8.63 us (5%)
  between operations  3.34 us (2%)
  other arithmetic  1.87 us (1%)
    pallas_call x1, Pallas kernels, squared(): pl.pallas_call(square_kernel, name='square_kernel', out_shape=jax.ShapeDt...  53.8 us
    pallas_call x1, Pallas kernels, tiles_in(): pl.pallas_call(tiles_in_kernel, name='tiles_in_kernel', out_shape=jax.Sha...  47.5 us
    pallas_call x1, Pallas kernels, tiles_back(): pl.pallas_call(tiles_back_kernel, name='tiles_back_kernel', out_shape=(ja...  45.2 us
    unnamed x10, local copies, waits for them, and re-layouts  8.54 us
    dot_general x1, matrix products, body(): jnp.dot(values.T, weighted, preferred_element_type=jnp.float32)  6.55 us
    dot_general x1, matrix products, body(): mixed = jnp.dot(values, submatrix, preferred_element_type=jnp.float32)  6.13 us

profile of v2, /device:TPU:0, one launch (start us, length us, event | category | flops | bytes accessed | tf_op | source)
XLA Modules:
  0.0 172.9 jit_solution(4763428856986927019)
XLA Ops:
  0.6 0.8 copy.17
  1.4 0.1 reshape.80.tiles_ref
  1.5 0.0 copy-start.1
  1.5 1.1 copy-done.1
  2.6 47.5 %tiles_in_kernel.1 = bf16[1024,1024]{1,0:T(8,128)(2,1)S(1)} custom-call(s32[1024]{0:T(1024)S(1)} %reshape.80.tiles_ref, bf16[6,128,384]{2,1,0:T(8,128)(2,1)S(1)} %bitcast.28), custom_call_target="tpu_custom_call" | custom-call | bytes 8388608 | tf_op jit(solution)/shard_map/tiles_in_kernel/pallas_call | solution.py:312
  50.0 4.6 %copy.18 = bf16[1,1536,1024]{1,2,0:T(8,128)(2,1)} copy(bf16[1,1536,1024]{2,1,0:T(8,128)(2,1)} %param.9) | data formatting | bytes 6291456 | tf_op args[0]
  54.7 0.0 copy-start.2
  54.7 6.1 %fusion = f32[1536]{0:T(1024)S(1)} fusion(bf16[1024,1024]{1,0:T(8,128)(2,1)S(1)} %tiles_in_kernel.1, bf16[1,1536,1024]{2,1,0:T(8,128)(2,1)} %param.9, bf16[1,1536,1024]{1,2,0:T(8,128)(2,1)} %copy.18), kind=kOutput, calls=%fused_computation.1 | convolution fusion | flops 3225942528 | bytes 8394752 | tf_op jit(solution)/shard_map/dot_general | solution.py:492
  61.5 0.6 compare_select_fusion
  62.1 0.0 copy-done.2
  62.1 0.0 copy-start
  62.2 6.6 %convert_bitcast_fusion.block_ref = bf16[1024,1024]{1,0:T(8,128)(2,1)S(1)} fusion(bf16[1,1536,1024]{2,1,0:T(8,128)(2,1)} %param.9, f32[1536]{0:T(1024)S(1)} %multiply_select_fusion), kind=kOutput, calls=%fused_computation.8 | convolution fusion | flops 3226992640 | bytes 5249024 | tf_op jit(solution)/shard_map/dot_general | solution.py:498
  68.7 0.8 add_bitcast_fusion
  69.5 0.2 select_reduce_fusion
  69.7 0.1 select_reduce_fusion.1
  71.1 0.1 pad_maximum_fusion.map_ref
  71.2 0.0 copy-done
  71.2 45.2 %tiles_back_kernel.1 = (f32[768,384]{1,0:T(8,128)S(1)}, f32[768,384]{1,0:T(8,128)S(1)}, bf16[768,384]{1,0:T(8,128)(2,1)S(1)}) custom-call(bf16[1024,1024]{1,0:T(8,128)(2,1)S(1)} %convert_bitcast_fusion.block_ref, s32[128]{0:T(128)S(1)} %compare_select_fusion.2.prev_ref, s32[36]{0:T(128)S(1)} %compare_select_fusion.1.last_ref, f32[2]{0:T(128)S(1)} %pad_maximum_fusion.map_ref, ...), custom_call_target="tpu_custom_call" | custom-call | bytes 16777216 | tf_op jit(solution)/shard_map/tiles_back_kernel/pallas_call | solution.py:430
  117.0 0.1 pad_maximum_fusion.1.mix_ref
  117.1 53.8 %square_kernel.1 = f32[768,384]{1,0:T(8,128)S(1)} custom-call(bf16[768,384]{1,0:T(8,128)(2,1)S(1)} %get-tuple-element.7.own_ref, f32[768,384]{1,0:T(8,128)S(1)} %get-tuple-element.8.start_ref, f32[2]{0:T(128)S(1)} %pad_maximum_fusion.1.mix_ref), custom_call_target="tpu_custom_call" | custom-call | flops 3623878656 | bytes 4718592 | tf_op jit(solution)/shard_map/square_kernel/pallas_call | solution.py:195
  170.9 1.0 copy.27
  171.9 1.0 copy.28
  (4 shorter events, 0.1 us)
Async XLA Ops:
  1.5 1.1 copy-start.1
  54.7 7.4 %copy-start.2 = (f32[1,1536]{1,0:T(1,128)S(1)}, f32[1,1536]{1,0:T(1,128)}, u32[]{:S(2)}) copy-start(f32[1,1536]{1,0:T(1,128)} %param.10) | copy-start | bytes 18436
  62.1 9.1 %copy-start = (f32[768,384]{1,0:T(8,128)S(1)}, f32[768,384]{1,0:T(8,128)}, u32[]{:S(2)}) copy-start(f32[768,384]{1,0:T(8,128)} %core_ref.1) | copy-start | bytes 3538948

commit v3 on v2

v3 whole, which is shorter than its diff:
```python
import jax
import jax.numpy as jnp
from jax import lax
from jax.experimental import pallas as pl
from jax.experimental.pallas import tpu as pltpu
from jax.sharding import PartitionSpec as P

MESH = pl.DeviceIdType.MESH
TILE = 128
PART = TILE // 2
BLK = 8
BS = 6
RING = 4
COLS = 16
DEVICES = 128
STRIDE = 37
SLATER = (3.0 / 3.141592653589793) ** (1.0 / 3.0)

def potential_factor(values):
    return -SLATER * (values * values + 1.0) ** (1.0 / 6.0)


def turn(value, step):
    return lax.rem(value + (step % RING), RING)


def offset_device(row, col, step):
    z, core = row // 2, lax.rem(row, 2)
    x, y = col // RING, lax.rem(col, RING)
    dx, dy = step // 32, lax.rem(step // 8, RING)
    dz, dcore = lax.rem(step // 2, RING), lax.rem(step, 2)
    there = lax.rem(z + dz, RING) * 2 + lax.rem(core + dcore, 2)
    return there, lax.rem(x + dx, RING) * RING + lax.rem(y + dy, RING)


CHUNK = 256
SLAB = 512


def greet_all(row, col):
    barrier = pltpu.get_barrier_semaphore()

    @pl.loop(1, DEVICES)
    def _(step):
        pl.semaphore_signal(barrier, inc=1, device_id=offset_device(row, col, step), device_id_type=MESH)

    pl.semaphore_wait(barrier, DEVICES - 1)


def square(
    row, col, own_ref, start_ref, scalar_ref, out_ref, rows_ref, cols_ref,
    row_send, row_recv, col_send, col_recv, core_send, core_recv, own_sem,
):
    z, core = row // 2, lax.rem(row, 2)
    x, y = col // RING, lax.rem(col, RING)
    tall, wide = own_ref.shape
    half = tall // 2
    quarter = half // 2

    def device(axis, step):
        if axis == "x":
            return (row, turn(x, step) * RING + y)
        if axis == "y":
            return (row, x * RING + turn(y, step))
        if axis == "z":
            return (turn(z, step) * 2 + core, col)
        return (z * 2 + 1 - core, col)

    def hop(place):
        position, part = place
        if position == 3:
            return 1, 0
        if position == 1:
            return -1, 0
        return (1, 3) if part == 0 else (-1, 1)

    def row_block(side, dx, dy):
        if dx == 0 and dy == 0:
            return own_ref.at[pl.ds(side * half, half)]
        return rows_ref.at[side, dx, dy]

    def row_copy(side, dx, dy, part=0):
        first, second = (dx, dy) if side == 0 else (dy, dx)
        axes = ("x", "y") if side == 0 else ("y", "x")
        place = second if second else first
        axis = axes[1] if second else axes[0]
        step, source = hop((place, part))
        origin = (first, source) if second else (source, 0)
        sx, sy = origin if side == 0 else origin[::-1]
        src, dst = row_block(side, sx, sy), rows_ref.at[side, dx, dy]
        if place == 2:
            cut = pl.ds(part * quarter, quarter)
            src, dst = src.at[cut], dst.at[cut]
        return pltpu.make_async_remote_copy(
            src_ref=src,
            dst_ref=dst,
            send_sem=row_send.at[side, dx, dy, part],
            recv_sem=row_recv.at[side, dx, dy, part],
            device_id=device(axis, step),
            device_id_type=MESH,
        )

    def col_copy(dz, part=0):
        step, source = hop((dz, part))
        slot = turn(z, source)
        src = own_ref if source == 0 else cols_ref.at[slot, core]
        dst = cols_ref.at[slot, core]
        if dz == 2:
            cut = pl.ds(part * half, half)
            src, dst = src.at[cut], dst.at[cut]
        return pltpu.make_async_remote_copy(
            src_ref=src,
            dst_ref=dst,
            send_sem=col_send.at[dz, part],
            recv_sem=col_recv.at[dz, part],
            device_id=device("z", step),
            device_id_type=MESH,
        )

    def core_copy(dz):
        slot = turn(z, dz)
        return pltpu.make_async_remote_copy(
            src_ref=own_ref if dz == 0 else cols_ref.at[slot, core],
            dst_ref=cols_ref.at[slot, core],
            send_sem=core_send.at[dz],
            recv_sem=core_recv.at[dz],
            device_id=device("core", 1),
            device_id_type=MESH,
        )

    def row_pair(side, first, second):
        return (first, second) if side == 0 else (second, first)

    started = []

    def go(copy):
        copy.start()
        started.append(copy)

    for place in (3, 1):
        for side in (0, 1):
            go(row_copy(side, *row_pair(side, place, 0)))
    for place in (3, 1):
        go(col_copy(place))
    go(core_copy(0))
    for place in (3, 1):
        for side in (0, 1):
            go(row_copy(side, *row_pair(side, 0, place)))
    mine = pltpu.make_async_copy(own_ref, cols_ref.at[z, core], own_sem)
    mine.start()

    for place, part in ((3, 0), (1, 1)):
        for side in (0, 1):
            row_copy(side, *row_pair(side, place, 0)).wait_recv()
            go(row_copy(side, *row_pair(side, 2, 0), part))
        for side in (0, 1):
            for second in (3, 1):
                go(row_copy(side, *row_pair(side, place, second)))
        col_copy(place).wait_recv()
        go(col_copy(2, part))
        go(core_copy(place))
    for side in (0, 1):
        for part in (0, 1):
            row_copy(side, *row_pair(side, 2, 0), part).wait_recv()
        for second in (3, 1):
            go(row_copy(side, *row_pair(side, 2, second)))
    for part in (0, 1):
        col_copy(2, part).wait_recv()
    go(core_copy(2))

    def second_ring(first):
        for place, part in ((3, 0), (1, 1)):
            for side in (0, 1):
                row_copy(side, *row_pair(side, first, place)).wait_recv()
                go(row_copy(side, *row_pair(side, first, 2), part))

    def multiply(side, dx, dy):
        index = turn(x, dx) * RING + turn(y, dy)
        owner, cut = index // 2, lax.rem(index, 2)
        factor = cols_ref[owner // 2, lax.rem(owner, 2), pl.ds(pl.multiple_of(cut * wide, wide), wide), :]
        product = jnp.dot(row_block(side, dx, dy)[...], factor, preferred_element_type=jnp.float32)
        spot = pl.ds(side * half, half)
        if dx == 0 and dy == 0:
            out_ref[spot, :] = product
        else:
            out_ref[spot, :] += product

    second_ring(0)
    mine.wait()
    for dz in range(RING):
        core_copy(dz).wait_recv()
    for side in (0, 1):
        for first in range(RING):
            multiply(side, *row_pair(side, first, 0))
        for place in (3, 1):
            multiply(side, *row_pair(side, 0, place))
    for first in (3, 1, 2):
        second_ring(first)
        for side in (0, 1):
            for place in (3, 1):
                multiply(side, *row_pair(side, first, place))
    for first in (0, 3, 1, 2):
        for side in (0, 1):
            for part in (0, 1):
                row_copy(side, *row_pair(side, first, 2), part).wait_recv()
            multiply(side, *row_pair(side, first, 2))
    out_ref[...] = scalar_ref[2] * out_ref[...] + scalar_ref[3] * start_ref[...]
    for copy in started:
        copy.wait_send()

def whole_kernel(
    tiles_ref,
    prev_ref,
    last_ref,
    scalar_ref,
    count_ref,
    weights_ref,
    dens_ref,
    basis_hbm,
    core_hbm,
    rho_ref,
    xc_ref,
    out_ref,
    basis_ref,
    core_ref,
    turned_ref,
    scaled_ref,
    both_ref,
    stage_ref,
    sub_ref,
    block_ref,
    landed_ref,
    sums_ref,
    give_ref,
    got_ref,
    start_ref,
    rounded_ref,
    rows_ref,
    cols_ref,
    load_sem,
    in_send,
    in_recv,
    in_own,
    back_send,
    back_recv,
    all_send,
    all_recv,
    row_send,
    row_recv,
    col_send,
    col_recv,
    core_send,
    core_recv,
    own_sem,
):
    row, col = lax.axis_index("row"), lax.axis_index("col")
    slot, side = col // 2, lax.rem(col, 2)
    other = 1 - side
    me = row * COLS + col
    partner = (row, slot * 2 + other)
    load_basis = pltpu.make_async_copy(basis_hbm, basis_ref, load_sem.at[0])
    load_core = pltpu.make_async_copy(core_hbm, core_ref, load_sem.at[1])
    load_basis.start()
    load_core.start()
    greet_all(row, col)

    pairs, mines = [], []
    for tile in range(BS // 2):
        cut = pl.ds(tile * TILE, TILE)
        spot = both_ref.at[pl.ds((side * (BS // 2) + tile) * BS, BS)]
        pairs.append(
            pltpu.make_async_remote_copy(
                src_ref=dens_ref.at[:, pl.ds(pl.multiple_of(other * PART, PART), PART), cut],
                dst_ref=spot,
                send_sem=in_send.at[tile],
                recv_sem=in_recv.at[tile],
                device_id=partner,
                device_id_type=MESH,
            )
        )
        mines.append(
            pltpu.make_async_copy(
                dens_ref.at[:, pl.ds(pl.multiple_of(side * PART, PART), PART), cut], spot, in_own.at[tile]
            )
        )
    for copy in pairs + mines:
        copy.start()
    for copy in mines + pairs:
        copy.wait()

    spot_rows = pl.ds(pl.multiple_of(row * TILE + side * PART, PART), PART)
    spot_cols = pl.ds(pl.multiple_of(slot * TILE, TILE), TILE)

    def stage(target):
        batch = target[0] * COLS + target[1]
        tile_row = tiles_ref[batch * BLK + row] - row * BS
        tile_col = tiles_ref[batch * BLK + slot] - slot * BS
        stage_ref[batch] = both_ref[jnp.clip(tile_col * BS + tile_row, 0, BS * BS - 1)]
        return batch

    @pl.loop(1, DEVICES)
    def _(count):
        target = offset_device(row, col, lax.rem(count * STRIDE, DEVICES))
        batch = stage(target)
        pltpu.make_async_remote_copy(
            src_ref=stage_ref.at[batch],
            dst_ref=sub_ref.at[spot_rows, spot_cols],
            send_sem=all_send.at[0],
            recv_sem=all_recv.at[0],
            device_id=target,
            device_id_type=MESH,
        ).start()

    stage((row, col))
    pltpu.make_async_copy(stage_ref.at[me], sub_ref.at[spot_rows, spot_cols], all_recv.at[0]).start()

    points, width = basis_ref.shape
    load_basis.wait()

    @pl.loop(0, points // CHUNK)
    def _(step):
        first = pl.multiple_of(step * CHUNK, CHUNK)
        turned_ref[:, pl.ds(first, CHUNK)] = basis_ref[pl.ds(first, CHUNK), :].T

    pltpu.make_async_copy(sub_ref, sub_ref, all_recv.at[0]).wait()

    @pl.loop(0, points // CHUNK)
    def _(step):
        cut = pl.ds(pl.multiple_of(step * CHUNK, CHUNK), CHUNK)
        mixed = jnp.dot(sub_ref[...], turned_ref[:, cut], preferred_element_type=jnp.float32)
        values = turned_ref[:, cut].astype(jnp.float32)
        density = jnp.sum(mixed * values, axis=0, keepdims=True)
        live = lax.broadcasted_iota(jnp.int32, density.shape, 1) + step * CHUNK < count_ref[0]
        density = jnp.where(live, density, jnp.float32(0.0))
        rho_ref[:, cut] = density
        factor = jnp.where(live, weights_ref[:, cut] * potential_factor(density), jnp.float32(0.0))
        scaled_ref[:, cut] = (factor * values).astype(jnp.bfloat16)

    @pl.loop(0, width // SLAB)
    def _(step):
        spot = pl.ds(pl.multiple_of(step * SLAB, SLAB), SLAB)
        block_ref[spot, :] = lax.dot_general(
            turned_ref[spot, :], scaled_ref[...], (((1,), (1,)), ((), ())), preferred_element_type=jnp.float32
        ).astype(jnp.bfloat16)

    def piece(target):
        there_row, there_col = target
        first = there_row * TILE + lax.rem(there_col, 2) * PART
        return block_ref.at[
            pl.ds(pl.multiple_of(first, PART), PART),
            pl.ds(pl.multiple_of(there_col // 2 * TILE, TILE), TILE),
        ]

    @pl.loop(1, DEVICES)
    def _(count):
        target = offset_device(row, col, lax.rem(count * STRIDE, DEVICES))
        pltpu.make_async_remote_copy(
            src_ref=piece(target),
            dst_ref=landed_ref.at[me],
            send_sem=all_send.at[1],
            recv_sem=all_recv.at[1],
            device_id=target,
            device_id_type=MESH,
        ).start()

    pltpu.make_async_copy(piece((row, col)), landed_ref.at[me], all_recv.at[1]).start()
    sums_ref[DEVICES] = jnp.zeros((PART, TILE), jnp.float32)
    rest = stage_ref.at[pl.ds(0, DEVICES - 1)]
    pltpu.make_async_copy(rest, rest, all_send.at[0]).wait()
    load_core.wait()
    pltpu.make_async_copy(landed_ref, landed_ref, all_recv.at[1]).wait()

    @pl.loop(0, DEVICES)
    def _(batch):
        sums_ref[batch] = sums_ref[prev_ref[batch]] + landed_ref[batch].astype(jnp.float32)

    def total(tile_row, half, tile):
        return sums_ref[last_ref[tile_row * BS + half * (BS // 2) + tile]]

    for tile_row in range(BS):
        for tile in range(BS // 2):
            cut = slice(tile * TILE, (tile + 1) * TILE)
            give_ref[tile_row, :, cut] = total(tile_row, other, tile).astype(give_ref.dtype)
    pair = pltpu.make_async_remote_copy(
        src_ref=give_ref,
        dst_ref=got_ref,
        send_sem=back_send,
        recv_sem=back_recv,
        device_id=partner,
        device_id_type=MESH,
    )
    pair.start()

    def finish(first, value):
        spot = pl.ds(pl.multiple_of(first, PART), PART)
        xc_ref[spot, :] = value
        down = lax.broadcasted_iota(jnp.int32, value.shape, 0) + (row * BS * TILE + first)
        across = lax.broadcasted_iota(jnp.int32, value.shape, 1) + col * xc_ref.shape[1]
        shift = jnp.where(down == across, scalar_ref[0], jnp.float32(0.0))
        start = shift + scalar_ref[1] * (core_ref[spot, :] + value)
        start_ref[spot, :] = start
        rounded_ref[spot, :] = start.astype(jnp.bfloat16)

    for tile_row in range(BS):
        mine = jnp.concatenate([total(tile_row, side, tile) for tile in range(BS // 2)], axis=1)
        finish(tile_row * TILE + side * PART, mine)
    pair.wait()
    for tile_row in range(BS):
        finish(tile_row * TILE + other * PART, got_ref[tile_row].astype(jnp.float32))

    square(
        row, col, rounded_ref, start_ref, scalar_ref, out_ref, rows_ref, cols_ref,
        row_send, row_recv, col_send, col_recv, core_send, core_recv, own_sem,
    )
    rest = landed_ref.at[pl.ds(0, DEVICES - 1)]
    pltpu.make_async_copy(rest, rest, all_send.at[1]).wait()


def whole(tiles, prev, last, scalars, count, weights, density, basis, core_matrix):
    dma = pltpu.SemaphoreType.DMA
    tall, wide = core_matrix.shape
    points, width = basis.shape
    vmem = pl.BlockSpec(memory_space=pltpu.VMEM)
    smem = pl.BlockSpec(memory_space=pltpu.SMEM)
    hbm = pl.BlockSpec(memory_space=pl.ANY)
    bf16, f32 = jnp.bfloat16, jnp.float32
    return pl.pallas_call(
        whole_kernel,
        name="whole_kernel",
        out_shape=(
            jax.ShapeDtypeStruct((1, points), f32),
            jax.ShapeDtypeStruct((tall, wide), f32),
            jax.ShapeDtypeStruct((tall, wide), f32),
        ),
        in_specs=[smem, smem, smem, smem, smem, vmem, vmem, hbm, hbm],
        out_specs=(vmem, vmem, vmem),
        scratch_shapes=[
            pltpu.VMEM((points, width), bf16),
            pltpu.VMEM((tall, wide), f32),
            pltpu.VMEM((width, points), bf16),
            pltpu.VMEM((width, points), bf16),
            pltpu.VMEM((BS * BS, PART, TILE), bf16),
            pltpu.VMEM((DEVICES, PART, TILE), bf16),
            pltpu.VMEM((width, width), bf16),
            pltpu.VMEM((width, width), bf16),
            pltpu.VMEM((DEVICES, PART, TILE), bf16),
            pltpu.VMEM((DEVICES + 1, PART, TILE), f32),
            pltpu.VMEM((BS, PART, wide), bf16),
            pltpu.VMEM((BS, PART, wide), bf16),
            pltpu.VMEM((tall, wide), f32),
            pltpu.VMEM((tall, wide), bf16),
            pltpu.VMEM((2, RING, RING, tall // 2, wide), bf16),
            pltpu.VMEM((RING, 2, tall, wide), bf16),
            dma((2,)),
            dma((BS // 2,)),
            dma((BS // 2,)),
            dma((BS // 2,)),
            dma,
            dma,
            dma((2,)),
            dma((2,)),
            dma((2, RING, RING, 2)),
            dma((2, RING, RING, 2)),
            dma((RING, 2)),
            dma((RING, 2)),
            dma((RING,)),
            dma((RING,)),
            dma,
        ],
        compiler_params=pltpu.CompilerParams(
            collective_id=1, has_side_effects=True, vmem_limit_bytes=56 * 2**20
        ),
        cost_estimate=pl.CostEstimate(
            flops=4 * points * width * width + 2 * tall * wide * tall * 8, bytes_accessed=16 * 2**20, transcendentals=0
        ),
    )(tiles.reshape(-1), prev, last, scalars, count, weights, density.reshape(BS, TILE, wide), basis, core_matrix)


def body(
    basis_values,
    quad_weights,
    point_counts,
    basis_tiles,
    density,
    core_matrix,
    map_shift,
    map_scale,
    branch_flags,
):
    row, col = lax.axis_index("row"), lax.axis_index("col")
    batches = jnp.arange(DEVICES, dtype=jnp.int32)
    down = lax.dynamic_index_in_dim(basis_tiles, row, 1, keepdims=False) - row * BS
    across = lax.dynamic_index_in_dim(basis_tiles, col // 2, 1, keepdims=False) - col // 2 * BS
    key = down * BS + across
    earlier = (key[:, None] == key[None, :]) & (batches[None, :] < batches[:, None])
    prev = jnp.max(jnp.where(earlier, batches[None, :], -1), axis=1)
    prev = jnp.where(prev < 0, DEVICES, prev)
    hits = jnp.arange(BS * BS, dtype=jnp.int32)[:, None] == key[None, :]
    last = jnp.max(jnp.where(hits, batches[None, :], -1), axis=1)
    last = jnp.where(last < 0, DEVICES, last)

    keep = branch_flags[0] == 0
    scalars = jnp.concatenate(
        [map_shift, map_scale, jnp.where(keep, 1.0, -1.0)[None], jnp.where(keep, 0.0, 2.0)[None]]
    ).astype(jnp.float32)
    local_density, potential, purified = whole(
        basis_tiles, prev, last, scalars, point_counts, quad_weights, density, basis_values[0], core_matrix
    )
    return (local_density, potential, purified)


def solution(mesh):
    placed = (
        P(("row", "col"), None, None),
        P(("row", "col"), None),
        P(("row", "col")),
        P(),
        P("row", "col"),
        P("row", "col"),
        P(),
        P(),
        P(),
    )
    return jax.shard_map(
        body,
        mesh=mesh,
        in_specs=placed,
        out_specs=(P(("row", "col"), None), P("row", "col"), P("row", "col")),
        check_vma=False,
    )
```

time: 173 us -> 160 us (0.925)
  matrix products: 12.7 us -> 0 us
  local copies, waits for them, and re-layouts: 8.63 us -> 6.23 us
    dot_general x2 -> x0, matrix products: 12.7 us -> none  [the longest x1 6.55 us: body(): jnp.dot(values.T, weighted, preferred_element_type=jnp.float32)]
    unnamed x10 -> x6, local copies, waits for them, and re-layouts: 8.54 us -> 5.54 us
    pallas_call x3 -> x1, Pallas kernels: 146 us -> 147 us  [whole(): pl.pallas_call(whole_kernel, name='whole_kernel', out_shape=(jax.ShapeDty...]
where the time goes in v3:
time: 160 us; the launch traced here: 159 us
  Pallas kernels  147 us (92%)
  local copies, waits for them, and re-layouts  6.23 us (4%)
  between operations  3.26 us (2%)
  other arithmetic  2.69 us (2%)
    pallas_call x1, Pallas kernels, whole(): pl.pallas_call(whole_kernel, name='whole_kernel', out_shape=(jax.ShapeDty...  147 us
    unnamed x6, local copies, waits for them, and re-layouts  5.54 us

profile of v3, /device:TPU:0, one launch (start us, length us, event | category | flops | bytes accessed | tf_op | source)
XLA Modules:
  0.0 159.0 jit_solution(2009628315143423232)
XLA Ops:
  3.2 0.6 pad_maximum_fusion.scalar_ref
  3.8 0.8 add_bitcast_fusion
  4.6 0.2 select_reduce_fusion
  4.8 0.1 select_reduce_fusion.1
  4.9 0.5 compare_select_fusion.last_ref
  5.4 0.5 compare_select_fusion.1.prev_ref
  5.9 0.8 copy.13
  6.7 0.7 reshape.41.tiles_ref
  7.4 146.9 %whole_kernel.1 = (f32[1,1536]{1,0:T(1,128)}, f32[768,384]{1,0:T(8,128)}, f32[768,384]{1,0:T(8,128)}) custom-call(s32[1024]{0:T(1024)} %reshape.41.tiles_ref, s32[128]{0:T(128)} %compare_select_fusion.1.prev_ref, s32[36]{0:T(128)} %compare_select_fusion.last_ref, f32[4]{0:T(128)} %pad_maximum_fusion.scalar_ref, s32[1]{0:T(128)S(6)} %copy.17.count_ref, ...), custom_call_target="tpu_custom_call" | custom-call | flops 10066329600 | bytes 16777216 | tf_op jit(solution)/shard_map/whole_kernel/pallas_call | solution.py:427
  154.3 1.3 copy.21
  155.6 0.0 copy-start
  155.6 2.5 %copy.22 = f32[768,384]{1,0:T(8,128)} copy(f32[768,384]{1,0:T(8,128)} %get-tuple-element.7) | data formatting | bytes 2359296
  158.0 0.0 copy-done
  158.0 1.0 copy.23
Async XLA Ops:
  155.6 2.5 %copy-start = (f32[768,384]{1,0:T(8,128)S(1)}, f32[768,384]{1,0:T(8,128)}, u32[]{:S(2)}) copy-start(f32[768,384]{1,0:T(8,128)} %get-tuple-element.8) | copy-start | bytes 3538948

commit v4 on v3

--- a/solution.py
+++ b/solution.py
@@ -37,18 +37,21 @@
 SLAB = 512
 
 
-def greet_all(row, col):
+def greet_all(me):
     barrier = pltpu.get_barrier_semaphore()
 
-    @pl.loop(1, DEVICES)
+    @pl.loop(1, DEVICES, unroll=8)
     def _(step):
-        pl.semaphore_signal(barrier, inc=1, device_id=offset_device(row, col, step), device_id_type=MESH)
-
-    pl.semaphore_wait(barrier, DEVICES - 1)
+        there = lax.rem(me + step, DEVICES)
+        pl.semaphore_signal(
+            barrier, inc=1, device_id=(there // COLS, lax.rem(there, COLS)), device_id_type=MESH
+        )
+
+    return barrier
 
 
 def square(
-    row, col, own_ref, start_ref, scalar_ref, out_ref, rows_ref, cols_ref,
+    row, col, own_ref, start_ref, flag_ref, out_ref, rows_ref, cols_ref,
     row_send, row_recv, col_send, col_recv, core_send, core_recv, own_sem,
 ):
     z, core = row // 2, lax.rem(row, 2)
@@ -204,20 +207,30 @@
             for part in (0, 1):
                 row_copy(side, *row_pair(side, first, 2), part).wait_recv()
             multiply(side, *row_pair(side, first, 2))
-    out_ref[...] = scalar_ref[2] * out_ref[...] + scalar_ref[3] * start_ref[...]
+    keep = flag_ref[0] == 0
+    sign = jnp.where(keep, 1.0, -1.0)
+    twice = jnp.where(keep, 0.0, 2.0)
+    out_ref[...] = sign * out_ref[...] + twice * start_ref[...]
     for copy in started:
         copy.wait_send()
 
 def whole_kernel(
-    tiles_ref,
-    prev_ref,
-    last_ref,
-    scalar_ref,
+    shift_ref,
+    scale_ref,
+    flag_ref,
     count_ref,
     weights_ref,
+    tiles_hbm,
     dens_ref,
     basis_hbm,
     core_hbm,
+    rho_hbm,
+    xc_hbm,
+    out_hbm,
+    tiles_ref,
+    tiles_vec,
+    chain_vec,
+    chain_ref,
     rho_ref,
     xc_ref,
     out_ref,
@@ -260,9 +273,15 @@
     partner = (row, slot * 2 + other)
     load_basis = pltpu.make_async_copy(basis_hbm, basis_ref, load_sem.at[0])
     load_core = pltpu.make_async_copy(core_hbm, core_ref, load_sem.at[1])
-    load_basis.start()
-    load_core.start()
-    greet_all(row, col)
+    load_tiles = [
+        pltpu.make_async_copy(tiles_hbm, tiles_ref, load_sem.at[2]),
+        pltpu.make_async_copy(tiles_hbm, tiles_vec, load_sem.at[3]),
+    ]
+    for copy in load_tiles:
+        copy.start()
+    barrier = greet_all(me)
+    for copy in load_tiles:
+        copy.wait()
 
     pairs, mines = [], []
     for tile in range(BS // 2):
@@ -283,8 +302,13 @@
                 dens_ref.at[:, pl.ds(pl.multiple_of(side * PART, PART), PART), cut], spot, in_own.at[tile]
             )
         )
-    for copy in pairs + mines:
+    for copy in mines:
         copy.start()
+    pl.semaphore_wait(barrier, DEVICES - 1)
+    for copy in pairs:
+        copy.start()
+    load_basis.start()
+    load_core.start()
     for copy in mines + pairs:
         copy.wait()
 
@@ -293,8 +317,8 @@
 
     def stage(target):
         batch = target[0] * COLS + target[1]
-        tile_row = tiles_ref[batch * BLK + row] - row * BS
-        tile_col = tiles_ref[batch * BLK + slot] - slot * BS
+        tile_row = tiles_ref[row, batch] - row * BS
+        tile_col = tiles_ref[slot, batch] - slot * BS
         stage_ref[batch] = both_ref[jnp.clip(tile_col * BS + tile_row, 0, BS * BS - 1)]
         return batch
 
@@ -314,6 +338,20 @@
     stage((row, col))
     pltpu.make_async_copy(stage_ref.at[me], sub_ref.at[spot_rows, spot_cols], all_recv.at[0]).start()
 
+    key = (tiles_vec[pl.ds(row, 1), :] - row * BS) * BS + tiles_vec[pl.ds(slot, 1), :] - slot * BS
+    across = jnp.broadcast_to(key, (DEVICES, DEVICES))
+    down = across.T
+    batch_down = lax.broadcasted_iota(jnp.int32, across.shape, 0)
+    batch_across = lax.broadcasted_iota(jnp.int32, across.shape, 1)
+    earlier = (down == across) & (batch_down < batch_across)
+    prev = jnp.max(jnp.where(earlier, batch_down, -1), axis=0, keepdims=True)
+    last = jnp.max(jnp.where(down == batch_across, batch_down, -1), axis=0, keepdims=True)
+    chain_vec[...] = jnp.zeros_like(chain_vec)
+    chain_vec[0:1, :] = jnp.where(prev < 0, DEVICES, prev)
+    chain_vec[1:2, :] = jnp.where(last < 0, DEVICES, last)
+    load_chain = pltpu.make_async_copy(chain_vec, chain_ref, load_sem.at[4])
+    load_chain.start()
+
     points, width = basis_ref.shape
     load_basis.wait()
 
@@ -368,14 +406,17 @@
     rest = stage_ref.at[pl.ds(0, DEVICES - 1)]
     pltpu.make_async_copy(rest, rest, all_send.at[0]).wait()
     load_core.wait()
+    load_chain.wait()
+    save_rho = pltpu.make_async_copy(rho_ref, rho_hbm, load_sem.at[0])
+    save_rho.start()
     pltpu.make_async_copy(landed_ref, landed_ref, all_recv.at[1]).wait()
 
     @pl.loop(0, DEVICES)
     def _(batch):
-        sums_ref[batch] = sums_ref[prev_ref[batch]] + landed_ref[batch].astype(jnp.float32)
+        sums_ref[batch] = sums_ref[chain_ref[0, batch]] + landed_ref[batch].astype(jnp.float32)
 
     def total(tile_row, half, tile):
-        return sums_ref[last_ref[tile_row * BS + half * (BS // 2) + tile]]
+        return sums_ref[chain_ref[1, tile_row * BS + half * (BS // 2) + tile]]
 
     for tile_row in range(BS):
         for tile in range(BS // 2):
@@ -396,8 +437,8 @@
         xc_ref[spot, :] = value
         down = lax.broadcasted_iota(jnp.int32, value.shape, 0) + (row * BS * TILE + first)
         across = lax.broadcasted_iota(jnp.int32, value.shape, 1) + col * xc_ref.shape[1]
-        shift = jnp.where(down == across, scalar_ref[0], jnp.float32(0.0))
-        start = shift + scalar_ref[1] * (core_ref[spot, :] + value)
+        shift = jnp.where(down == across, shift_ref[0], jnp.float32(0.0))
+        start = shift + scale_ref[0] * (core_ref[spot, :] + value)
         start_ref[spot, :] = start
         rounded_ref[spot, :] = start.astype(jnp.bfloat16)
 
@@ -408,15 +449,23 @@
     for tile_row in range(BS):
         finish(tile_row * TILE + other * PART, got_ref[tile_row].astype(jnp.float32))
 
+    save_xc = pltpu.make_async_copy(xc_ref, xc_hbm, load_sem.at[1])
+    save_xc.start()
+
     square(
-        row, col, rounded_ref, start_ref, scalar_ref, out_ref, rows_ref, cols_ref,
+        row, col, rounded_ref, start_ref, flag_ref, out_ref, rows_ref, cols_ref,
         row_send, row_recv, col_send, col_recv, core_send, core_recv, own_sem,
     )
     rest = landed_ref.at[pl.ds(0, DEVICES - 1)]
     pltpu.make_async_copy(rest, rest, all_send.at[1]).wait()
-
-
-def whole(tiles, prev, last, scalars, count, weights, density, basis, core_matrix):
+    save_out = pltpu.make_async_copy(out_ref, out_hbm, load_sem.at[2])
+    save_out.start()
+    save_rho.wait()
+    save_xc.wait()
+    save_out.wait()
+
+
+def whole(shift, scale, flag, count, weights, tiles, density, basis, core_matrix):
     dma = pltpu.SemaphoreType.DMA
     tall, wide = core_matrix.shape
     points, width = basis.shape
@@ -432,9 +481,16 @@
             jax.ShapeDtypeStruct((tall, wide), f32),
             jax.ShapeDtypeStruct((tall, wide), f32),
         ),
-        in_specs=[smem, smem, smem, smem, smem, vmem, vmem, hbm, hbm],
-        out_specs=(vmem, vmem, vmem),
+        in_specs=[smem, smem, smem, smem, vmem, hbm, hbm, hbm, hbm],
+        out_specs=(hbm, hbm, hbm),
         scratch_shapes=[
+            pltpu.SMEM((BLK, DEVICES), jnp.int32),
+            pltpu.VMEM((BLK, DEVICES), jnp.int32),
+            pltpu.VMEM((BLK, DEVICES), jnp.int32),
+            pltpu.SMEM((BLK, DEVICES), jnp.int32),
+            pltpu.VMEM((1, points), f32),
+            pltpu.VMEM((tall, wide), f32),
+            pltpu.VMEM((tall, wide), f32),
             pltpu.VMEM((points, width), bf16),
             pltpu.VMEM((tall, wide), f32),
             pltpu.VMEM((width, points), bf16),
@@ -451,7 +507,7 @@
             pltpu.VMEM((tall, wide), bf16),
             pltpu.VMEM((2, RING, RING, tall // 2, wide), bf16),
             pltpu.VMEM((RING, 2, tall, wide), bf16),
-            dma((2,)),
+            dma((5,)),
             dma((BS // 2,)),
             dma((BS // 2,)),
             dma((BS // 2,)),
@@ -473,7 +529,36 @@
         cost_estimate=pl.CostEstimate(
             flops=4 * points * width * width + 2 * tall * wide * tall * 8, bytes_accessed=16 * 2**20, transcendentals=0
         ),
-    )(tiles.reshape(-1), prev, last, scalars, count, weights, density.reshape(BS, TILE, wide), basis, core_matrix)
+    )(shift, scale, flag, count, weights, tiles, density.reshape(BS, TILE, wide), basis, core_matrix)
+
+
+def keep_kernel(*refs):
+    count = (len(refs) - 1) // 3
+    sems = refs[-1]
+    loads, saves = [], []
+    for i in range(count):
+        source, target, held = refs[i], refs[count + i], refs[2 * count + i]
+        loads.append(pltpu.make_async_copy(source, held, sems.at[0, i]))
+        saves.append(pltpu.make_async_copy(held, target, sems.at[1, i]))
+    for load in loads:
+        load.start()
+    for load, save in zip(loads, saves):
+        load.wait()
+        save.start()
+    for save in saves:
+        save.wait()
+
+
+def kept(*arrays):
+    hbm = pl.BlockSpec(memory_space=pl.ANY)
+    return pl.pallas_call(
+        keep_kernel,
+        name="keep_kernel",
+        out_shape=tuple(jax.ShapeDtypeStruct(a.shape, a.dtype) for a in arrays),
+        in_specs=[hbm] * len(arrays),
+        out_specs=(hbm,) * len(arrays),
+        scratch_shapes=[pltpu.VMEM(a.shape, a.dtype) for a in arrays] + [pltpu.SemaphoreType.DMA((2, len(arrays)))],
+    )(*arrays)
 
 
 def body(
@@ -487,26 +572,19 @@
     map_scale,
     branch_flags,
 ):
-    row, col = lax.axis_index("row"), lax.axis_index("col")
-    batches = jnp.arange(DEVICES, dtype=jnp.int32)
-    down = lax.dynamic_index_in_dim(basis_tiles, row, 1, keepdims=False) - row * BS
-    across = lax.dynamic_index_in_dim(basis_tiles, col // 2, 1, keepdims=False) - col // 2 * BS
-    key = down * BS + across
-    earlier = (key[:, None] == key[None, :]) & (batches[None, :] < batches[:, None])
-    prev = jnp.max(jnp.where(earlier, batches[None, :], -1), axis=1)
-    prev = jnp.where(prev < 0, DEVICES, prev)
-    hits = jnp.arange(BS * BS, dtype=jnp.int32)[:, None] == key[None, :]
-    last = jnp.max(jnp.where(hits, batches[None, :], -1), axis=1)
-    last = jnp.where(last < 0, DEVICES, last)
-
-    keep = branch_flags[0] == 0
-    scalars = jnp.concatenate(
-        [map_shift, map_scale, jnp.where(keep, 1.0, -1.0)[None], jnp.where(keep, 0.0, 2.0)[None]]
-    ).astype(jnp.float32)
-    local_density, potential, purified = whole(
-        basis_tiles, prev, last, scalars, point_counts, quad_weights, density, basis_values[0], core_matrix
+    return kept(
+        *whole(
+            map_shift,
+            map_scale,
+            branch_flags,
+            point_counts,
+            quad_weights,
+            basis_tiles.T,
+            density,
+            basis_values[0],
+            core_matrix,
+        )
     )
-    return (local_density, potential, purified)
 
 
 def solution(mesh):

time: 160 us -> 150 us (0.938)
  local copies, waits for them, and re-layouts: 6.23 us -> 0 us
  other arithmetic: 2.69 us -> 0 us
    unnamed x6 -> x0, local copies, waits for them, and re-layouts: 5.54 us -> none
    pallas_call x1, Pallas kernels: 147 us -> 144 us  [whole(): pl.pallas_call(whole_kernel, name='whole_kernel', out_shape=(jax.ShapeDty...]
    pallas_call x0 -> x1, Pallas kernels: none -> 2.74 us  [kept(): pl.pallas_call(keep_kernel, name='keep_kernel', out_shape=tuple((jax.Shap...]
where the time goes in v4:
time: 150 us; the launch traced here: 149 us
  Pallas kernels  146 us (97%)
  between operations  3.22 us (2%)
    pallas_call x1, Pallas kernels, whole(): pl.pallas_call(whole_kernel, name='whole_kernel', out_shape=(jax.ShapeDty...  144 us

profile of v4, /device:TPU:0, one launch (start us, length us, event | category | flops | bytes accessed | tf_op | source)
XLA Modules:
  0.0 149.5 jit_solution(9281472038034046862)
XLA Ops:
  3.2 143.5 %whole_kernel.1 = (f32[1,1536]{1,0:T(1,128)}, f32[768,384]{1,0:T(8,128)}, f32[768,384]{1,0:T(8,128)}) custom-call(f32[1]{0:T(128)S(6)} %copy.13.shift_ref, f32[1]{0:T(128)S(6)} %copy.14.scale_ref, s32[1]{0:T(128)S(6)} %copy.15.flag_ref, s32[1]{0:T(128)S(6)} %copy.12.count_ref, f32[1,1536]{1,0:T(1,128)} %weights_ref.1, s32[8,128]{1,0:T(8,128)} %bitcast.5, ...), custom_call_target="tpu_custom_call" | custom-call | flops 10066329600 | bytes 16777216 | tf_op jit(solution)/shard_map/whole_kernel/pallas_call | solution.py:476
  146.7 2.7 %keep_kernel.1 = (f32[1,1536]{1,0:T(1,128)}, f32[768,384]{1,0:T(8,128)}, f32[768,384]{1,0:T(8,128)}) custom-call(f32[1,1536]{1,0:T(1,128)} %get-tuple-element.6.refs_0_, f32[768,384]{1,0:T(8,128)} %get-tuple-element.7.refs_1_, f32[768,384]{1,0:T(8,128)} %get-tuple-element.8.refs_2_), custom_call_target="tpu_custom_call" | custom-call | tf_op jit(solution)/shard_map/keep_kernel/pallas_call | solution.py:554

commit v5 on v4

--- a/solution.py
+++ b/solution.py
@@ -50,169 +50,14 @@
     return barrier
 
 
-def square(
-    row, col, own_ref, start_ref, flag_ref, out_ref, rows_ref, cols_ref,
-    row_send, row_recv, col_send, col_recv, core_send, core_recv, own_sem,
-):
-    z, core = row // 2, lax.rem(row, 2)
-    x, y = col // RING, lax.rem(col, RING)
-    tall, wide = own_ref.shape
-    half = tall // 2
-    quarter = half // 2
-
-    def device(axis, step):
-        if axis == "x":
-            return (row, turn(x, step) * RING + y)
-        if axis == "y":
-            return (row, x * RING + turn(y, step))
-        if axis == "z":
-            return (turn(z, step) * 2 + core, col)
-        return (z * 2 + 1 - core, col)
-
-    def hop(place):
-        position, part = place
-        if position == 3:
-            return 1, 0
-        if position == 1:
-            return -1, 0
-        return (1, 3) if part == 0 else (-1, 1)
-
-    def row_block(side, dx, dy):
-        if dx == 0 and dy == 0:
-            return own_ref.at[pl.ds(side * half, half)]
-        return rows_ref.at[side, dx, dy]
-
-    def row_copy(side, dx, dy, part=0):
-        first, second = (dx, dy) if side == 0 else (dy, dx)
-        axes = ("x", "y") if side == 0 else ("y", "x")
-        place = second if second else first
-        axis = axes[1] if second else axes[0]
-        step, source = hop((place, part))
-        origin = (first, source) if second else (source, 0)
-        sx, sy = origin if side == 0 else origin[::-1]
-        src, dst = row_block(side, sx, sy), rows_ref.at[side, dx, dy]
-        if place == 2:
-            cut = pl.ds(part * quarter, quarter)
-            src, dst = src.at[cut], dst.at[cut]
-        return pltpu.make_async_remote_copy(
-            src_ref=src,
-            dst_ref=dst,
-            send_sem=row_send.at[side, dx, dy, part],
-            recv_sem=row_recv.at[side, dx, dy, part],
-            device_id=device(axis, step),
-            device_id_type=MESH,
-        )
-
-    def col_copy(dz, part=0):
-        step, source = hop((dz, part))
-        slot = turn(z, source)
-        src = own_ref if source == 0 else cols_ref.at[slot, core]
-        dst = cols_ref.at[slot, core]
-        if dz == 2:
-            cut = pl.ds(part * half, half)
-            src, dst = src.at[cut], dst.at[cut]
-        return pltpu.make_async_remote_copy(
-            src_ref=src,
-            dst_ref=dst,
-            send_sem=col_send.at[dz, part],
-            recv_sem=col_recv.at[dz, part],
-            device_id=device("z", step),
-            device_id_type=MESH,
-        )
-
-    def core_copy(dz):
-        slot = turn(z, dz)
-        return pltpu.make_async_remote_copy(
-            src_ref=own_ref if dz == 0 else cols_ref.at[slot, core],
-            dst_ref=cols_ref.at[slot, core],
-            send_sem=core_send.at[dz],
-            recv_sem=core_recv.at[dz],
-            device_id=device("core", 1),
-            device_id_type=MESH,
-        )
-
-    def row_pair(side, first, second):
-        return (first, second) if side == 0 else (second, first)
-
-    started = []
-
-    def go(copy):
-        copy.start()
-        started.append(copy)
-
-    for place in (3, 1):
-        for side in (0, 1):
-            go(row_copy(side, *row_pair(side, place, 0)))
-    for place in (3, 1):
-        go(col_copy(place))
-    go(core_copy(0))
-    for place in (3, 1):
-        for side in (0, 1):
-            go(row_copy(side, *row_pair(side, 0, place)))
-    mine = pltpu.make_async_copy(own_ref, cols_ref.at[z, core], own_sem)
-    mine.start()
-
-    for place, part in ((3, 0), (1, 1)):
-        for side in (0, 1):
-            row_copy(side, *row_pair(side, place, 0)).wait_recv()
-            go(row_copy(side, *row_pair(side, 2, 0), part))
-        for side in (0, 1):
-            for second in (3, 1):
-                go(row_copy(side, *row_pair(side, place, second)))
-        col_copy(place).wait_recv()
-        go(col_copy(2, part))
-        go(core_copy(place))
-    for side in (0, 1):
-        for part in (0, 1):
-            row_copy(side, *row_pair(side, 2, 0), part).wait_recv()
-        for second in (3, 1):
-            go(row_copy(side, *row_pair(side, 2, second)))
-    for part in (0, 1):
-        col_copy(2, part).wait_recv()
-    go(core_copy(2))
-
-    def second_ring(first):
-        for place, part in ((3, 0), (1, 1)):
-            for side in (0, 1):
-                row_copy(side, *row_pair(side, first, place)).wait_recv()
-                go(row_copy(side, *row_pair(side, first, 2), part))
-
-    def multiply(side, dx, dy):
-        index = turn(x, dx) * RING + turn(y, dy)
-        owner, cut = index // 2, lax.rem(index, 2)
-        factor = cols_ref[owner // 2, lax.rem(owner, 2), pl.ds(pl.multiple_of(cut * wide, wide), wide), :]
-        product = jnp.dot(row_block(side, dx, dy)[...], factor, preferred_element_type=jnp.float32)
-        spot = pl.ds(side * half, half)
-        if dx == 0 and dy == 0:
-            out_ref[spot, :] = product
-        else:
-            out_ref[spot, :] += product
-
-    second_ring(0)
-    mine.wait()
-    for dz in range(RING):
-        core_copy(dz).wait_recv()
-    for side in (0, 1):
-        for first in range(RING):
-            multiply(side, *row_pair(side, first, 0))
-        for place in (3, 1):
-            multiply(side, *row_pair(side, 0, place))
-    for first in (3, 1, 2):
-        second_ring(first)
-        for side in (0, 1):
-            for place in (3, 1):
-                multiply(side, *row_pair(side, first, place))
-    for first in (0, 3, 1, 2):
-        for side in (0, 1):
-            for part in (0, 1):
-                row_copy(side, *row_pair(side, first, 2), part).wait_recv()
-            multiply(side, *row_pair(side, first, 2))
-    keep = flag_ref[0] == 0
-    sign = jnp.where(keep, 1.0, -1.0)
-    twice = jnp.where(keep, 0.0, 2.0)
-    out_ref[...] = sign * out_ref[...] + twice * start_ref[...]
-    for copy in started:
-        copy.wait_send()
+def hop(place):
+    position, part = place
+    if position == 3:
+        return 1, 0
+    if position == 1:
+        return -1, 0
+    return (1, 3) if part == 0 else (-1, 1)
+
 
 def whole_kernel(
     shift_ref,
@@ -244,18 +89,24 @@
     block_ref,
     landed_ref,
     sums_ref,
+    band_ref,
+    own_ref,
+    depth_ref,
     give_ref,
     got_ref,
-    start_ref,
-    rounded_ref,
-    rows_ref,
+    piece_ref,
     cols_ref,
+    total_ref,
+    give_total_ref,
+    got_total_ref,
     load_sem,
     in_send,
     in_recv,
     in_own,
-    back_send,
-    back_recv,
+    swap_send,
+    swap_recv,
+    total_send,
+    total_recv,
     all_send,
     all_recv,
     row_send,
@@ -273,6 +124,20 @@
     partner = (row, slot * 2 + other)
     load_basis = pltpu.make_async_copy(basis_hbm, basis_ref, load_sem.at[0])
     load_core = pltpu.make_async_copy(core_hbm, core_ref, load_sem.at[1])
+    half_wide = core_hbm.shape[2]
+    near_cols = pl.ds(pl.multiple_of(side * half_wide, half_wide), half_wide)
+    far_cols = pl.ds(pl.multiple_of(other * half_wide, half_wide), half_wide)
+    near_part = pl.ds(pl.multiple_of(side * PART, PART), PART)
+    far_part = pl.ds(pl.multiple_of(other * PART, PART), PART)
+    mine_core = pltpu.make_async_copy(core_hbm.at[:, near_part], band_ref.at[:, :, near_cols], load_sem.at[5])
+    swap_core = pltpu.make_async_remote_copy(
+        src_ref=core_hbm.at[:, far_part],
+        dst_ref=band_ref.at[:, :, near_cols],
+        send_sem=swap_send.at[0],
+        recv_sem=swap_recv.at[0],
+        device_id=partner,
+        device_id_type=MESH,
+    )
     load_tiles = [
         pltpu.make_async_copy(tiles_hbm, tiles_ref, load_sem.at[2]),
         pltpu.make_async_copy(tiles_hbm, tiles_vec, load_sem.at[3]),
@@ -309,6 +174,7 @@
         copy.start()
     load_basis.start()
     load_core.start()
+    mine_core.start()
     for copy in mines + pairs:
         copy.wait()
 
@@ -361,6 +227,7 @@
         turned_ref[:, pl.ds(first, CHUNK)] = basis_ref[pl.ds(first, CHUNK), :].T
 
     pltpu.make_async_copy(sub_ref, sub_ref, all_recv.at[0]).wait()
+    swap_core.start()
 
     @pl.loop(0, points // CHUNK)
     def _(step):
@@ -415,51 +282,234 @@
     def _(batch):
         sums_ref[batch] = sums_ref[chain_ref[0, batch]] + landed_ref[batch].astype(jnp.float32)
 
-    def total(tile_row, half, tile):
-        return sums_ref[chain_ref[1, tile_row * BS + half * (BS // 2) + tile]]
-
+    def total(tile_row, tile):
+        return sums_ref[chain_ref[1, tile_row * BS + tile]]
+
+    mine_core.wait()
+    swap_core.wait()
+    wide = BS * TILE
     for tile_row in range(BS):
-        for tile in range(BS // 2):
-            cut = slice(tile * TILE, (tile + 1) * TILE)
-            give_ref[tile_row, :, cut] = total(tile_row, other, tile).astype(give_ref.dtype)
+        value = jnp.concatenate([total(tile_row, tile) for tile in range(BS)], axis=1)
+        down = lax.broadcasted_iota(jnp.int32, value.shape, 0) + (row * wide + tile_row * TILE + side * PART)
+        across = lax.broadcasted_iota(jnp.int32, value.shape, 1) + slot * wide
+        shift = jnp.where(down == across, shift_ref[0], jnp.float32(0.0))
+        start = shift + scale_ref[0] * (band_ref[tile_row] + value)
+        band_ref[tile_row] = start
+        spot = slice(tile_row * PART, (tile_row + 1) * PART)
+        own_ref[spot, :] = start.astype(jnp.bfloat16)
+        for depth in (0, 1):
+            lanes = [start[:, tile * TILE + depth * PART : tile * TILE + (depth + 1) * PART] for tile in range(BS)]
+            depth_ref[depth, spot, :] = jnp.concatenate(lanes, axis=1).astype(jnp.bfloat16)
+
+    z, core = row // 2, lax.rem(row, 2)
+    x, y = col // RING, lax.rem(col, RING)
+    piece_rows = own_ref.shape[0]
+
+    def device(axis, step):
+        if axis == "x":
+            return (row, turn(x, step) * RING + y)
+        if axis == "y":
+            return (row, x * RING + turn(y, step))
+        if axis == "z":
+            return (turn(z, step) * 2 + core, col)
+        return (z * 2 + 1 - core, col)
+
+    def piece_at(dx, dy):
+        if dx == 0 and dy == 0:
+            return depth_ref.at[side]
+        return piece_ref.at[dx, dy]
+
+    def y_copy(dy):
+        step = -dy
+        return pltpu.make_async_remote_copy(
+            src_ref=depth_ref.at[side if dy == 2 else other],
+            dst_ref=piece_ref.at[0, dy],
+            send_sem=row_send.at[0, dy, 0],
+            recv_sem=row_recv.at[0, dy, 0],
+            device_id=device("y", step),
+            device_id_type=MESH,
+        )
+
+    def x_copy(dx, dy, part=0):
+        step, source = hop((dx, part))
+        src, dst = piece_at(source, dy), piece_ref.at[dx, dy]
+        if dx == 2:
+            part_rows = pl.ds(part * (piece_rows // 2), piece_rows // 2)
+            src, dst = src.at[part_rows], dst.at[part_rows]
+        return pltpu.make_async_remote_copy(
+            src_ref=src,
+            dst_ref=dst,
+            send_sem=row_send.at[dx, dy, part],
+            recv_sem=row_recv.at[dx, dy, part],
+            device_id=device("x", step),
+            device_id_type=MESH,
+        )
+
+    def z_copy(dz, part=0):
+        step, source = hop((dz, part))
+        place = turn(z, source)
+        src = own_ref if source == 0 else cols_ref.at[place, core]
+        dst = cols_ref.at[place, core]
+        if dz == 2:
+            part_rows = pl.ds(part * (piece_rows // 2), piece_rows // 2)
+            src, dst = src.at[part_rows], dst.at[part_rows]
+        return pltpu.make_async_remote_copy(
+            src_ref=src,
+            dst_ref=dst,
+            send_sem=col_send.at[dz, part],
+            recv_sem=col_recv.at[dz, part],
+            device_id=device("z", step),
+            device_id_type=MESH,
+        )
+
+    def core_copy(dz):
+        place = turn(z, dz)
+        return pltpu.make_async_remote_copy(
+            src_ref=own_ref if dz == 0 else cols_ref.at[place, core],
+            dst_ref=cols_ref.at[place, core],
+            send_sem=core_send.at[dz],
+            recv_sem=core_recv.at[dz],
+            device_id=device("core", 1),
+            device_id_type=MESH,
+        )
+
+    started = []
+
+    def go(copy):
+        copy.start()
+        started.append(copy)
+
+    for dx in (3, 1):
+        go(x_copy(dx, 0))
+    for dy in (2, 3, 1):
+        go(y_copy(dy))
+    for dz in (3, 1):
+        go(z_copy(dz))
+    go(core_copy(0))
+    mine = pltpu.make_async_copy(own_ref, cols_ref.at[z, core], own_sem)
+    mine.start()
+
+    def strip(tile_row, half):
+        found = [sums_ref[chain_ref[1, tile_row * BS + half * (BS // 2) + tile]] for tile in range(BS // 2)]
+        return jnp.concatenate(found, axis=1)
+
+    for tile_row in range(BS):
+        give_ref[tile_row] = strip(tile_row, other)
     pair = pltpu.make_async_remote_copy(
         src_ref=give_ref,
         dst_ref=got_ref,
-        send_sem=back_send,
-        recv_sem=back_recv,
+        send_sem=swap_send.at[1],
+        recv_sem=swap_recv.at[1],
         device_id=partner,
         device_id_type=MESH,
     )
-    pair.start()
-
-    def finish(first, value):
-        spot = pl.ds(pl.multiple_of(first, PART), PART)
-        xc_ref[spot, :] = value
-        down = lax.broadcasted_iota(jnp.int32, value.shape, 0) + (row * BS * TILE + first)
-        across = lax.broadcasted_iota(jnp.int32, value.shape, 1) + col * xc_ref.shape[1]
-        shift = jnp.where(down == across, shift_ref[0], jnp.float32(0.0))
-        start = shift + scale_ref[0] * (core_ref[spot, :] + value)
-        start_ref[spot, :] = start
-        rounded_ref[spot, :] = start.astype(jnp.bfloat16)
-
+    go(pair)
     for tile_row in range(BS):
-        mine = jnp.concatenate([total(tile_row, side, tile) for tile in range(BS // 2)], axis=1)
-        finish(tile_row * TILE + side * PART, mine)
-    pair.wait()
+        xc_ref[pl.ds(pl.multiple_of(tile_row * TILE + side * PART, PART), PART), :] = strip(tile_row, side)
+
+    def pass_on(dy):
+        for dx, part in ((3, 0), (1, 1)):
+            x_copy(dx, dy).wait_recv()
+            go(x_copy(2, dy, part))
+
+    pass_on(0)
+    for dy in (2, 3, 1):
+        y_copy(dy).wait_recv()
+        for dx in (3, 1):
+            go(x_copy(dx, dy))
+    for dz, part in ((3, 0), (1, 1)):
+        z_copy(dz).wait_recv()
+        go(z_copy(2, part))
+        go(core_copy(dz))
+    pass_on(2)
+    for part in (0, 1):
+        z_copy(2, part).wait_recv()
+    go(core_copy(2))
+
+    def multiply(dx, dy):
+        there_x, there_y = turn(x, dx), turn(y, dy)
+        factor = cols_ref[there_x, there_y // 2]
+        product = jnp.dot(piece_at(dx, dy)[...], factor, preferred_element_type=jnp.float32)
+        group = dy % 2
+        if dx == 0 and dy in (0, 3):
+            total_ref[group] = product
+        else:
+            total_ref[group] += product
+
+    def swap_total(group):
+        kind = side if group == 0 else other
+        give_total_ref[group] = total_ref[group, :, far_cols].astype(jnp.bfloat16)
+        return pltpu.make_async_remote_copy(
+            src_ref=give_total_ref.at[group],
+            dst_ref=got_total_ref.at[kind],
+            send_sem=total_send.at[group],
+            recv_sem=total_recv.at[kind],
+            device_id=partner,
+            device_id_type=MESH,
+        )
+
+    mine.wait()
+    for dz in range(RING):
+        core_copy(dz).wait_recv()
+    multiply(0, 0)
+    for dx in (3, 1):
+        multiply(dx, 0)
+    for part in (0, 1):
+        x_copy(2, 0, part).wait_recv()
+    multiply(2, 0)
+    for dx in (0, 3, 1):
+        multiply(dx, 2)
+    pass_on(3)
+    for part in (0, 1):
+        x_copy(2, 2, part).wait_recv()
+    multiply(2, 2)
+    go(swap_total(0))
+    for dx in (0, 3, 1):
+        multiply(dx, 3)
+    multiply(0, 1)
+    pair.wait_recv()
     for tile_row in range(BS):
-        finish(tile_row * TILE + other * PART, got_ref[tile_row].astype(jnp.float32))
-
+        xc_ref[pl.ds(pl.multiple_of(tile_row * TILE + other * PART, PART), PART), :] = got_ref[tile_row]
     save_xc = pltpu.make_async_copy(xc_ref, xc_hbm, load_sem.at[1])
     save_xc.start()
-
-    square(
-        row, col, rounded_ref, start_ref, flag_ref, out_ref, rows_ref, cols_ref,
-        row_send, row_recv, col_send, col_recv, core_send, core_recv, own_sem,
-    )
+    pass_on(1)
+    for dx in (3, 1):
+        multiply(dx, 1)
+    for dy in (3, 1):
+        for part in (0, 1):
+            x_copy(2, dy, part).wait_recv()
+        multiply(2, dy)
+    go(swap_total(1))
+
+    keep = flag_ref[0] == 0
+    sign = jnp.where(keep, 1.0, -1.0)
+    twice = jnp.where(keep, 0.0, 2.0)
+
+    def finish(group):
+        kind = side if group == 0 else other
+        got = pltpu.make_async_copy(got_total_ref.at[kind], got_total_ref.at[kind], total_recv.at[kind])
+        got.wait()
+        for tile_row in range(BS):
+            spot = slice(tile_row * PART, (tile_row + 1) * PART)
+            first = pl.multiple_of(tile_row * TILE + kind * PART, PART)
+            if group == 0:
+                start = band_ref[tile_row, :, near_cols]
+            else:
+                down = lax.broadcasted_iota(jnp.int32, (PART, half_wide), 0) + (row * wide + first)
+                across = lax.broadcasted_iota(jnp.int32, (PART, half_wide), 1) + col * half_wide
+                shift = jnp.where(down == across, shift_ref[0], jnp.float32(0.0))
+                start = shift + scale_ref[0] * (core_ref[tile_row, far_part] + xc_ref[pl.ds(first, PART), :])
+            square = total_ref[group, spot, near_cols] + got_total_ref[kind, spot, :].astype(jnp.float32)
+            out_ref[pl.ds(first, PART), :] = sign * square + twice * start
+
+    finish(1)
+    finish(0)
+    save_out = pltpu.make_async_copy(out_ref, out_hbm, load_sem.at[2])
+    save_out.start()
+    for copy in started:
+        copy.wait_send()
     rest = landed_ref.at[pl.ds(0, DEVICES - 1)]
     pltpu.make_async_copy(rest, rest, all_send.at[1]).wait()
-    save_out = pltpu.make_async_copy(out_ref, out_hbm, load_sem.at[2])
-    save_out.start()
     save_rho.wait()
     save_xc.wait()
     save_out.wait()
@@ -492,7 +542,7 @@
             pltpu.VMEM((tall, wide), f32),
             pltpu.VMEM((tall, wide), f32),
             pltpu.VMEM((points, width), bf16),
-            pltpu.VMEM((tall, wide), f32),
+            pltpu.VMEM((BS, TILE, wide), f32),
             pltpu.VMEM((width, points), bf16),
             pltpu.VMEM((width, points), bf16),
             pltpu.VMEM((BS * BS, PART, TILE), bf16),
@@ -501,22 +551,28 @@
             pltpu.VMEM((width, width), bf16),
             pltpu.VMEM((DEVICES, PART, TILE), bf16),
             pltpu.VMEM((DEVICES + 1, PART, TILE), f32),
-            pltpu.VMEM((BS, PART, wide), bf16),
-            pltpu.VMEM((BS, PART, wide), bf16),
-            pltpu.VMEM((tall, wide), f32),
-            pltpu.VMEM((tall, wide), bf16),
-            pltpu.VMEM((2, RING, RING, tall // 2, wide), bf16),
-            pltpu.VMEM((RING, 2, tall, wide), bf16),
-            dma((5,)),
+            pltpu.VMEM((BS, PART, 2 * wide), f32),
+            pltpu.VMEM((BS * PART, 2 * wide), bf16),
+            pltpu.VMEM((2, BS * PART, wide), bf16),
+            pltpu.VMEM((BS, PART, wide), f32),
+            pltpu.VMEM((BS, PART, wide), f32),
+            pltpu.VMEM((RING, RING, BS * PART, wide), bf16),
+            pltpu.VMEM((RING, 2, BS * PART, 2 * wide), bf16),
+            pltpu.VMEM((2, BS * PART, 2 * wide), f32),
+            pltpu.VMEM((2, BS * PART, wide), bf16),
+            pltpu.VMEM((2, BS * PART, wide), bf16),
+            dma((6,)),
             dma((BS // 2,)),
             dma((BS // 2,)),
             dma((BS // 2,)),
-            dma,
-            dma,
             dma((2,)),
             dma((2,)),
-            dma((2, RING, RING, 2)),
-            dma((2, RING, RING, 2)),
+            dma((2,)),
+            dma((2,)),
+            dma((2,)),
+            dma((2,)),
+            dma((RING, RING, 2)),
+            dma((RING, RING, 2)),
             dma((RING, 2)),
             dma((RING, 2)),
             dma((RING,)),
@@ -529,7 +585,7 @@
         cost_estimate=pl.CostEstimate(
             flops=4 * points * width * width + 2 * tall * wide * tall * 8, bytes_accessed=16 * 2**20, transcendentals=0
         ),
-    )(shift, scale, flag, count, weights, tiles, density.reshape(BS, TILE, wide), basis, core_matrix)
+    )(shift, scale, flag, count, weights, tiles, density.reshape(BS, TILE, wide), basis, core_matrix.reshape(BS, TILE, wide))
 
 
 def keep_kernel(*refs):

time: 150 us -> 145 us (0.967)
  Pallas kernels: 146 us -> 141 us
    pallas_call x1, Pallas kernels: 144 us -> 139 us  [whole(): pl.pallas_call(whole_kernel, name='whole_kernel', out_shape=(jax.ShapeDty...]
where the time goes in v5:
time: 145 us
  Pallas kernels  141 us (97%)
  between operations  3.22 us (2%)
    pallas_call x1, Pallas kernels, whole(): pl.pallas_call(whole_kernel, name='whole_kernel', out_shape=(jax.ShapeDty...  139 us

profile of v5, /device:TPU:0, one launch (start us, length us, event | category | flops | bytes accessed | tf_op | source)
XLA Modules:
  0.0 144.6 jit_solution(2515682175806621395)
XLA Ops:
  3.2 138.6 %whole_kernel.1 = (f32[1,1536]{1,0:T(1,128)}, f32[768,384]{1,0:T(8,128)}, f32[768,384]{1,0:T(8,128)}) custom-call(f32[1]{0:T(128)S(6)} %copy.13.shift_ref, f32[1]{0:T(128)S(6)} %copy.14.scale_ref, s32[1]{0:T(128)S(6)} %copy.15.flag_ref, s32[1]{0:T(128)S(6)} %copy.12.count_ref, f32[1,1536]{1,0:T(1,128)} %weights_ref.1, s32[8,128]{1,0:T(8,128)} %bitcast.7, ...), custom_call_target="tpu_custom_call" | custom-call | flops 10066329600 | bytes 16777216 | tf_op jit(solution)/shard_map/whole_kernel/pallas_call | solution.py:526
  141.8 2.7 %keep_kernel.1 = (f32[1,1536]{1,0:T(1,128)}, f32[768,384]{1,0:T(8,128)}, f32[768,384]{1,0:T(8,128)}) custom-call(f32[1,1536]{1,0:T(1,128)} %get-tuple-element.6.refs_0_, f32[768,384]{1,0:T(8,128)} %get-tuple-element.7.refs_1_, f32[768,384]{1,0:T(8,128)} %get-tuple-element.8.refs_2_), custom_call_target="tpu_custom_call" | custom-call | tf_op jit(solution)/shard_map/keep_kernel/pallas_call | solution.py:610

commit v6 on v5

--- a/solution.py
+++ b/solution.py
@@ -24,17 +24,19 @@
     return lax.rem(value + (step % RING), RING)
 
 
-def offset_device(row, col, step):
+def offset_device(row, col, half, count):
+    step = lax.rem(count * STRIDE, DEVICES // 2)
     z, core = row // 2, lax.rem(row, 2)
     x, y = col // RING, lax.rem(col, RING)
-    dx, dy = step // 32, lax.rem(step // 8, RING)
-    dz, dcore = lax.rem(step // 2, RING), lax.rem(step, 2)
+    dx, dy = step // 16, lax.rem(step // 4, RING)
+    dz, dcore = half + lax.rem(step // 2, 2) * 2, lax.rem(step, 2)
     there = lax.rem(z + dz, RING) * 2 + lax.rem(core + dcore, 2)
     return there, lax.rem(x + dx, RING) * RING + lax.rem(y + dy, RING)
 
 
 CHUNK = 256
-SLAB = 512
+STEPS = 32767.0
+JOBS = ((0, 0, 192), (0, 192, 192), (3, 0, 384), (1, 0, 384), (2, 0, 256), (2, 256, 128))
 
 
 def greet_all(me):
@@ -92,6 +94,10 @@
     band_ref,
     own_ref,
     depth_ref,
+    give_core_ref,
+    got_core_ref,
+    give_most_ref,
+    got_most_ref,
     give_ref,
     got_ref,
     piece_ref,
@@ -109,8 +115,12 @@
     total_recv,
     all_send,
     all_recv,
+    in_halves,
     row_send,
     row_recv,
+    y_send,
+    y_recv,
+    save_sem,
     col_send,
     col_recv,
     core_send,
@@ -131,10 +141,18 @@
     far_part = pl.ds(pl.multiple_of(other * PART, PART), PART)
     mine_core = pltpu.make_async_copy(core_hbm.at[:, near_part], band_ref.at[:, :, near_cols], load_sem.at[5])
     swap_core = pltpu.make_async_remote_copy(
-        src_ref=core_hbm.at[:, far_part],
-        dst_ref=band_ref.at[:, :, near_cols],
+        src_ref=give_core_ref,
+        dst_ref=got_core_ref,
         send_sem=swap_send.at[0],
         recv_sem=swap_recv.at[0],
+        device_id=partner,
+        device_id_type=MESH,
+    )
+    swap_most = pltpu.make_async_remote_copy(
+        src_ref=give_most_ref,
+        dst_ref=got_most_ref,
+        send_sem=swap_send.at[2],
+        recv_sem=swap_recv.at[2],
         device_id=partner,
         device_id_type=MESH,
     )
@@ -172,14 +190,18 @@
     pl.semaphore_wait(barrier, DEVICES - 1)
     for copy in pairs:
         copy.start()
+    load_core.start()
     load_basis.start()
-    load_core.start()
     mine_core.start()
     for copy in mines + pairs:
         copy.wait()
 
-    spot_rows = pl.ds(pl.multiple_of(row * TILE + side * PART, PART), PART)
+    depth_z, depth_core = row // 2, lax.rem(row, 2)
     spot_cols = pl.ds(pl.multiple_of(slot * TILE, TILE), TILE)
+
+    def landing(half):
+        first = (depth_z // 2) * 2 * TILE + depth_core * TILE + side * PART
+        return sub_ref.at[half, pl.ds(pl.multiple_of(first, PART), PART), spot_cols]
 
     def stage(target):
         batch = target[0] * COLS + target[1]
@@ -188,21 +210,24 @@
         stage_ref[batch] = both_ref[jnp.clip(tile_col * BS + tile_row, 0, BS * BS - 1)]
         return batch
 
-    @pl.loop(1, DEVICES)
-    def _(count):
-        target = offset_device(row, col, lax.rem(count * STRIDE, DEVICES))
-        batch = stage(target)
-        pltpu.make_async_remote_copy(
-            src_ref=stage_ref.at[batch],
-            dst_ref=sub_ref.at[spot_rows, spot_cols],
-            send_sem=all_send.at[0],
-            recv_sem=all_recv.at[0],
-            device_id=target,
-            device_id_type=MESH,
-        ).start()
-
-    stage((row, col))
-    pltpu.make_async_copy(stage_ref.at[me], sub_ref.at[spot_rows, spot_cols], all_recv.at[0]).start()
+    for half in (0, 1):
+
+        @pl.loop(1 - half, DEVICES // 2)
+        def _(count, half=half):
+            target = offset_device(row, col, half, count)
+            batch = stage(target)
+            pltpu.make_async_remote_copy(
+                src_ref=stage_ref.at[batch],
+                dst_ref=landing(half),
+                send_sem=all_send.at[0],
+                recv_sem=in_halves.at[half],
+                device_id=target,
+                device_id_type=MESH,
+            ).start()
+
+        if half == 0:
+            stage((row, col))
+            pltpu.make_async_copy(stage_ref.at[me], landing(0), in_halves.at[0]).start()
 
     key = (tiles_vec[pl.ds(row, 1), :] - row * BS) * BS + tiles_vec[pl.ds(slot, 1), :] - slot * BS
     across = jnp.broadcast_to(key, (DEVICES, DEVICES))
@@ -218,6 +243,17 @@
     load_chain = pltpu.make_async_copy(chain_vec, chain_ref, load_sem.at[4])
     load_chain.start()
 
+    load_core.wait()
+    most = jnp.zeros((1, 1), jnp.float32)
+    for tile_row in range(BS):
+        strip_most = jnp.max(jnp.abs(core_ref[tile_row, far_part]), axis=0, keepdims=True)
+        most = jnp.maximum(most, jnp.max(strip_most, axis=1, keepdims=True))
+    most = jnp.maximum(most, 1e-30)
+    give_most_ref[...] = jnp.broadcast_to(most, give_most_ref.shape)
+    for tile_row in range(BS):
+        steps = jnp.round(core_ref[tile_row, far_part] * (STEPS / most))
+        give_core_ref[tile_row] = steps.astype(jnp.int32).astype(jnp.int16)
+
     points, width = basis_ref.shape
     load_basis.wait()
 
@@ -226,27 +262,35 @@
         first = pl.multiple_of(step * CHUNK, CHUNK)
         turned_ref[:, pl.ds(first, CHUNK)] = basis_ref[pl.ds(first, CHUNK), :].T
 
-    pltpu.make_async_copy(sub_ref, sub_ref, all_recv.at[0]).wait()
-    swap_core.start()
-
-    @pl.loop(0, points // CHUNK)
-    def _(step):
-        cut = pl.ds(pl.multiple_of(step * CHUNK, CHUNK), CHUNK)
-        mixed = jnp.dot(sub_ref[...], turned_ref[:, cut], preferred_element_type=jnp.float32)
-        values = turned_ref[:, cut].astype(jnp.float32)
-        density = jnp.sum(mixed * values, axis=0, keepdims=True)
-        live = lax.broadcasted_iota(jnp.int32, density.shape, 1) + step * CHUNK < count_ref[0]
-        density = jnp.where(live, density, jnp.float32(0.0))
-        rho_ref[:, cut] = density
-        factor = jnp.where(live, weights_ref[:, cut] * potential_factor(density), jnp.float32(0.0))
-        scaled_ref[:, cut] = (factor * values).astype(jnp.bfloat16)
-
-    @pl.loop(0, width // SLAB)
-    def _(step):
-        spot = pl.ds(pl.multiple_of(step * SLAB, SLAB), SLAB)
-        block_ref[spot, :] = lax.dot_general(
-            turned_ref[spot, :], scaled_ref[...], (((1,), (1,)), ((), ())), preferred_element_type=jnp.float32
-        ).astype(jnp.bfloat16)
+    def band(half, which):
+        place = which * 2 + lax.rem(depth_z + half, 2)
+        return pl.ds(pl.multiple_of(place * 2 * TILE, 2 * TILE), 2 * TILE)
+
+    for half in (0, 1):
+        landed_half = pltpu.make_async_copy(sub_ref.at[half], sub_ref.at[half], in_halves.at[half])
+        landed_half.wait()
+        if half == 1:
+            swap_core.start()
+            swap_most.start()
+
+        @pl.loop(0, points // CHUNK)
+        def _(step, half=half):
+            cut = pl.ds(pl.multiple_of(step * CHUNK, CHUNK), CHUNK)
+            mixed = jnp.dot(sub_ref[half], turned_ref[:, cut], preferred_element_type=jnp.float32)
+            density = jnp.zeros((1, CHUNK), jnp.float32)
+            for which in (0, 1):
+                values = turned_ref[band(half, which), cut].astype(jnp.float32)
+                part = mixed[which * 2 * TILE : (which + 1) * 2 * TILE]
+                density += jnp.sum(part * values, axis=0, keepdims=True)
+            if half == 0:
+                rho_ref[:, cut] = density
+                return
+            density += rho_ref[:, cut]
+            live = lax.broadcasted_iota(jnp.int32, density.shape, 1) + step * CHUNK < count_ref[0]
+            density = jnp.where(live, density, jnp.float32(0.0))
+            rho_ref[:, cut] = density
+            factor = jnp.where(live, weights_ref[:, cut] * potential_factor(density), jnp.float32(0.0))
+            scaled_ref[:, cut] = (factor * turned_ref[:, cut].astype(jnp.float32)).astype(jnp.bfloat16)
 
     def piece(target):
         there_row, there_col = target
@@ -256,23 +300,33 @@
             pl.ds(pl.multiple_of(there_col // 2 * TILE, TILE), TILE),
         ]
 
-    @pl.loop(1, DEVICES)
-    def _(count):
-        target = offset_device(row, col, lax.rem(count * STRIDE, DEVICES))
-        pltpu.make_async_remote_copy(
-            src_ref=piece(target),
-            dst_ref=landed_ref.at[me],
-            send_sem=all_send.at[1],
-            recv_sem=all_recv.at[1],
-            device_id=target,
-            device_id_type=MESH,
-        ).start()
-
-    pltpu.make_async_copy(piece((row, col)), landed_ref.at[me], all_recv.at[1]).start()
+    for half in (0, 1):
+        bands = [band(half, 0), band(half, 1)]
+        values = jnp.concatenate([turned_ref[spot, :] for spot in bands], axis=0)
+        result = lax.dot_general(
+            values, scaled_ref[...], (((1,), (1,)), ((), ())), preferred_element_type=jnp.float32
+        ).astype(jnp.bfloat16)
+        for which in (0, 1):
+            block_ref[bands[which], :] = result[which * 2 * TILE : (which + 1) * 2 * TILE]
+
+        @pl.loop(1 - half, DEVICES // 2)
+        def _(count, half=half):
+            target = offset_device(row, col, half, count)
+            pltpu.make_async_remote_copy(
+                src_ref=piece(target),
+                dst_ref=landed_ref.at[me],
+                send_sem=all_send.at[1],
+                recv_sem=all_recv.at[1],
+                device_id=target,
+                device_id_type=MESH,
+            ).start()
+
+        if half == 0:
+            pltpu.make_async_copy(piece((row, col)), landed_ref.at[me], all_recv.at[1]).start()
+
     sums_ref[DEVICES] = jnp.zeros((PART, TILE), jnp.float32)
     rest = stage_ref.at[pl.ds(0, DEVICES - 1)]
     pltpu.make_async_copy(rest, rest, all_send.at[0]).wait()
-    load_core.wait()
     load_chain.wait()
     save_rho = pltpu.make_async_copy(rho_ref, rho_hbm, load_sem.at[0])
     save_rho.start()
@@ -287,12 +341,15 @@
 
     mine_core.wait()
     swap_core.wait()
+    swap_most.wait()
+    most = got_most_ref[0:1, 0:1] / STEPS
     wide = BS * TILE
     for tile_row in range(BS):
         value = jnp.concatenate([total(tile_row, tile) for tile in range(BS)], axis=1)
         down = lax.broadcasted_iota(jnp.int32, value.shape, 0) + (row * wide + tile_row * TILE + side * PART)
         across = lax.broadcasted_iota(jnp.int32, value.shape, 1) + slot * wide
         shift = jnp.where(down == across, shift_ref[0], jnp.float32(0.0))
+        band_ref[tile_row, :, far_cols] = got_core_ref[tile_row].astype(jnp.int32).astype(jnp.float32) * most
         start = shift + scale_ref[0] * (band_ref[tile_row] + value)
         band_ref[tile_row] = start
         spot = slice(tile_row * PART, (tile_row + 1) * PART)
@@ -324,23 +381,23 @@
         return pltpu.make_async_remote_copy(
             src_ref=depth_ref.at[side if dy == 2 else other],
             dst_ref=piece_ref.at[0, dy],
-            send_sem=row_send.at[0, dy, 0],
-            recv_sem=row_recv.at[0, dy, 0],
+            send_sem=y_send.at[dy],
+            recv_sem=y_recv.at[dy],
             device_id=device("y", step),
             device_id_type=MESH,
         )
 
-    def x_copy(dx, dy, part=0):
+    def x_copy(job, dx, part=0):
+        dy, first, count = JOBS[job]
         step, source = hop((dx, part))
-        src, dst = piece_at(source, dy), piece_ref.at[dx, dy]
         if dx == 2:
-            part_rows = pl.ds(part * (piece_rows // 2), piece_rows // 2)
-            src, dst = src.at[part_rows], dst.at[part_rows]
+            first, count = first + part * (count // 2), count // 2
+        spot = pl.ds(first, count)
         return pltpu.make_async_remote_copy(
-            src_ref=src,
-            dst_ref=dst,
-            send_sem=row_send.at[dx, dy, part],
-            recv_sem=row_recv.at[dx, dy, part],
+            src_ref=piece_at(source, dy).at[spot],
+            dst_ref=piece_ref.at[dx, dy].at[spot],
+            send_sem=row_send.at[job, dx, part],
+            recv_sem=row_recv.at[job, dx, part],
             device_id=device("x", step),
             device_id_type=MESH,
         )
@@ -379,9 +436,22 @@
         copy.start()
         started.append(copy)
 
-    for dx in (3, 1):
-        go(x_copy(dx, 0))
-    for dy in (2, 3, 1):
+    def start_job(job):
+        for dx in (3, 1):
+            go(x_copy(job, dx))
+
+    def pass_on(job):
+        for dx, part in ((3, 0), (1, 1)):
+            x_copy(job, dx).wait_recv()
+            go(x_copy(job, 2, part))
+
+    def far_landed(job):
+        for part in (0, 1):
+            x_copy(job, 2, part).wait_recv()
+
+    start_job(0)
+    start_job(1)
+    for dy in (3, 1, 2):
         go(y_copy(dy))
     for dz in (3, 1):
         go(z_copy(dz))
@@ -403,116 +473,142 @@
         device_id=partner,
         device_id_type=MESH,
     )
-    go(pair)
     for tile_row in range(BS):
         xc_ref[pl.ds(pl.multiple_of(tile_row * TILE + side * PART, PART), PART), :] = strip(tile_row, side)
 
-    def pass_on(dy):
-        for dx, part in ((3, 0), (1, 1)):
-            x_copy(dx, dy).wait_recv()
-            go(x_copy(2, dy, part))
-
     pass_on(0)
-    for dy in (2, 3, 1):
-        y_copy(dy).wait_recv()
-        for dx in (3, 1):
-            go(x_copy(dx, dy))
+    y_copy(3).wait_recv()
+    start_job(2)
+    pass_on(1)
+    y_copy(1).wait_recv()
+    start_job(3)
     for dz, part in ((3, 0), (1, 1)):
         z_copy(dz).wait_recv()
         go(z_copy(2, part))
         go(core_copy(dz))
+    y_copy(2).wait_recv()
+    go(pair)
     pass_on(2)
+    start_job(4)
     for part in (0, 1):
         z_copy(2, part).wait_recv()
     go(core_copy(2))
 
-    def multiply(dx, dy):
+    def multiply(job, dx):
+        dy, first, count = JOBS[job]
+        spot = pl.ds(first, count)
         there_x, there_y = turn(x, dx), turn(y, dy)
         factor = cols_ref[there_x, there_y // 2]
-        product = jnp.dot(piece_at(dx, dy)[...], factor, preferred_element_type=jnp.float32)
+        product = jnp.dot(piece_at(dx, dy)[spot, :], factor, preferred_element_type=jnp.float32)
         group = dy % 2
         if dx == 0 and dy in (0, 3):
-            total_ref[group] = product
+            total_ref[group, spot, :] = product
         else:
-            total_ref[group] += product
-
-    def swap_total(group):
+            total_ref[group, spot, :] += product
+
+    cuts = ((1, 0, 384), (0, 0, 256), (0, 256, 128))
+
+    def swap_total(event):
+        group, first, count = cuts[event]
         kind = side if group == 0 else other
-        give_total_ref[group] = total_ref[group, :, far_cols].astype(jnp.bfloat16)
+        spot = pl.ds(first, count)
         return pltpu.make_async_remote_copy(
-            src_ref=give_total_ref.at[group],
-            dst_ref=got_total_ref.at[kind],
-            send_sem=total_send.at[group],
-            recv_sem=total_recv.at[kind],
+            src_ref=give_total_ref.at[group, spot],
+            dst_ref=got_total_ref.at[kind, spot],
+            send_sem=total_send.at[event],
+            recv_sem=total_recv.at[event],
             device_id=partner,
             device_id_type=MESH,
         )
+
+    def hand_over(event):
+        group, first, count = cuts[event]
+        spot = pl.ds(first, count)
+        give_total_ref[group, spot, :] = total_ref[group, spot, far_cols].astype(jnp.bfloat16)
+        go(swap_total(event))
+
+    keep = flag_ref[0] == 0
+    sign = jnp.where(keep, 1.0, -1.0)
+    twice = jnp.where(keep, 0.0, 2.0)
+    saves = []
+
+    def finish(group, first_row, count):
+        kind = side if group == 0 else other
+        kind_part = near_part if group == 0 else far_part
+        for tile_row in range(first_row // PART, (first_row + count) // PART):
+            spot = slice(tile_row * PART, (tile_row + 1) * PART)
+            if group == 0:
+                start = band_ref[tile_row, :, near_cols]
+            else:
+                first = tile_row * TILE + kind * PART
+                down = lax.broadcasted_iota(jnp.int32, (PART, half_wide), 0) + (row * wide + first)
+                across = lax.broadcasted_iota(jnp.int32, (PART, half_wide), 1) + col * half_wide
+                shift = jnp.where(down == across, shift_ref[0], jnp.float32(0.0))
+                start = shift + scale_ref[0] * (core_ref[tile_row, far_part] + got_ref[tile_row])
+            square = total_ref[group, spot, near_cols] + got_total_ref[kind, spot, :].astype(jnp.float32)
+            out_ref[tile_row, kind_part] = sign * square + twice * start
+        tile_rows = pl.ds(first_row // PART, count // PART)
+        save = pltpu.make_async_copy(
+            out_ref.at[tile_rows, kind_part], out_hbm.at[tile_rows, kind_part], save_sem.at[len(saves)]
+        )
+        save.start()
+        saves.append(save)
 
     mine.wait()
     for dz in range(RING):
         core_copy(dz).wait_recv()
-    multiply(0, 0)
+    for job in (0, 1):
+        multiply(job, 0)
+    pass_on(3)
+    start_job(5)
+    for job in (2, 3):
+        multiply(job, 0)
+    for job in (0, 1):
+        far_landed(job)
+        for dx in (3, 1, 2):
+            multiply(job, dx)
     for dx in (3, 1):
-        multiply(dx, 0)
-    for part in (0, 1):
-        x_copy(2, 0, part).wait_recv()
-    multiply(2, 0)
+        multiply(2, dx)
+    far_landed(2)
+    multiply(2, 2)
+    for dx in (3, 1):
+        multiply(3, dx)
+    far_landed(3)
+    multiply(3, 2)
+    hand_over(0)
+    pass_on(4)
     for dx in (0, 3, 1):
-        multiply(dx, 2)
-    pass_on(3)
-    for part in (0, 1):
-        x_copy(2, 2, part).wait_recv()
-    multiply(2, 2)
-    go(swap_total(0))
-    for dx in (0, 3, 1):
-        multiply(dx, 3)
-    multiply(0, 1)
+        multiply(4, dx)
     pair.wait_recv()
     for tile_row in range(BS):
         xc_ref[pl.ds(pl.multiple_of(tile_row * TILE + other * PART, PART), PART), :] = got_ref[tile_row]
     save_xc = pltpu.make_async_copy(xc_ref, xc_hbm, load_sem.at[1])
     save_xc.start()
-    pass_on(1)
+    multiply(5, 0)
+    far_landed(4)
+    multiply(4, 2)
+    hand_over(1)
+    pass_on(5)
     for dx in (3, 1):
-        multiply(dx, 1)
-    for dy in (3, 1):
-        for part in (0, 1):
-            x_copy(2, dy, part).wait_recv()
-        multiply(2, dy)
-    go(swap_total(1))
-
-    keep = flag_ref[0] == 0
-    sign = jnp.where(keep, 1.0, -1.0)
-    twice = jnp.where(keep, 0.0, 2.0)
-
-    def finish(group):
-        kind = side if group == 0 else other
-        got = pltpu.make_async_copy(got_total_ref.at[kind], got_total_ref.at[kind], total_recv.at[kind])
-        got.wait()
-        for tile_row in range(BS):
-            spot = slice(tile_row * PART, (tile_row + 1) * PART)
-            first = pl.multiple_of(tile_row * TILE + kind * PART, PART)
-            if group == 0:
-                start = band_ref[tile_row, :, near_cols]
-            else:
-                down = lax.broadcasted_iota(jnp.int32, (PART, half_wide), 0) + (row * wide + first)
-                across = lax.broadcasted_iota(jnp.int32, (PART, half_wide), 1) + col * half_wide
-                shift = jnp.where(down == across, shift_ref[0], jnp.float32(0.0))
-                start = shift + scale_ref[0] * (core_ref[tile_row, far_part] + xc_ref[pl.ds(first, PART), :])
-            square = total_ref[group, spot, near_cols] + got_total_ref[kind, spot, :].astype(jnp.float32)
-            out_ref[pl.ds(first, PART), :] = sign * square + twice * start
-
-    finish(1)
-    finish(0)
-    save_out = pltpu.make_async_copy(out_ref, out_hbm, load_sem.at[2])
-    save_out.start()
+        multiply(5, dx)
+    swap_total(0).wait_recv()
+    finish(0, 0, 256)
+    far_landed(5)
+    multiply(5, 2)
+    hand_over(2)
+    finish(0, 256, 128)
+    swap_total(1).wait_recv()
+    finish(1, 0, 256)
+    swap_total(2).wait_recv()
+    finish(1, 256, 128)
     for copy in started:
         copy.wait_send()
     rest = landed_ref.at[pl.ds(0, DEVICES - 1)]
     pltpu.make_async_copy(rest, rest, all_send.at[1]).wait()
     save_rho.wait()
     save_xc.wait()
-    save_out.wait()
+    for save in saves:
+        save.wait()
 
 
 def whole(shift, scale, flag, count, weights, tiles, density, basis, core_matrix):
@@ -529,7 +625,7 @@
         out_shape=(
             jax.ShapeDtypeStruct((1, points), f32),
             jax.ShapeDtypeStruct((tall, wide), f32),
-            jax.ShapeDtypeStruct((tall, wide), f32),
+            jax.ShapeDtypeStruct((BS, TILE, wide), f32),
         ),
         in_specs=[smem, smem, smem, smem, vmem, hbm, hbm, hbm, hbm],
         out_specs=(hbm, hbm, hbm),
@@ -540,20 +636,24 @@
             pltpu.SMEM((BLK, DEVICES), jnp.int32),
             pltpu.VMEM((1, points), f32),
             pltpu.VMEM((tall, wide), f32),
-            pltpu.VMEM((tall, wide), f32),
+            pltpu.VMEM((BS, TILE, wide), f32),
             pltpu.VMEM((points, width), bf16),
             pltpu.VMEM((BS, TILE, wide), f32),
             pltpu.VMEM((width, points), bf16),
             pltpu.VMEM((width, points), bf16),
             pltpu.VMEM((BS * BS, PART, TILE), bf16),
             pltpu.VMEM((DEVICES, PART, TILE), bf16),
-            pltpu.VMEM((width, width), bf16),
+            pltpu.VMEM((2, width // 2, width), bf16),
             pltpu.VMEM((width, width), bf16),
             pltpu.VMEM((DEVICES, PART, TILE), bf16),
             pltpu.VMEM((DEVICES + 1, PART, TILE), f32),
             pltpu.VMEM((BS, PART, 2 * wide), f32),
             pltpu.VMEM((BS * PART, 2 * wide), bf16),
             pltpu.VMEM((2, BS * PART, wide), bf16),
+            pltpu.VMEM((BS, PART, wide), jnp.int16),
+            pltpu.VMEM((BS, PART, wide), jnp.int16),
+            pltpu.VMEM((8, TILE), f32),
+            pltpu.VMEM((8, TILE), f32),
             pltpu.VMEM((BS, PART, wide), f32),
             pltpu.VMEM((BS, PART, wide), f32),
             pltpu.VMEM((RING, RING, BS * PART, wide), bf16),
@@ -565,14 +665,18 @@
             dma((BS // 2,)),
             dma((BS // 2,)),
             dma((BS // 2,)),
+            dma((3,)),
+            dma((3,)),
+            dma((3,)),
+            dma((3,)),
             dma((2,)),
             dma((2,)),
             dma((2,)),
-            dma((2,)),
-            dma((2,)),
-            dma((2,)),
-            dma((RING, RING, 2)),
-            dma((RING, RING, 2)),
+            dma((len(JOBS), RING, 2)),
+            dma((len(JOBS), RING, 2)),
+            dma((RING,)),
+            dma((RING,)),
+            dma((4,)),
             dma((RING, 2)),
             dma((RING, 2)),
             dma((RING,)),
@@ -628,19 +732,18 @@
     map_scale,
     branch_flags,
 ):
-    return kept(
-        *whole(
-            map_shift,
-            map_scale,
-            branch_flags,
-            point_counts,
-            quad_weights,
-            basis_tiles.T,
-            density,
-            basis_values[0],
-            core_matrix,
-        )
+    density_out, potential, purified = whole(
+        map_shift,
+        map_scale,
+        branch_flags,
+        point_counts,
+        quad_weights,
+        basis_tiles.T,
+        density,
+        basis_values[0],
+        core_matrix,
     )
+    return kept(density_out, potential, purified.reshape(core_matrix.shape))
 
 
 def solution(mesh):

time: 145 us -> 138 us (0.952)
  Pallas kernels: 141 us -> 134 us
    pallas_call x1, Pallas kernels: 139 us -> 132 us  [whole(): pl.pallas_call(whole_kernel, name='whole_kernel', out_shape=(jax.ShapeDty...]
where the time goes in v6:
time: 138 us
  Pallas kernels  134 us (97%)
  between operations  3.22 us (2%)
    pallas_call x1, Pallas kernels, whole(): pl.pallas_call(whole_kernel, name='whole_kernel', out_shape=(jax.ShapeDty...  132 us

profile of v6, /device:TPU:0, one launch (start us, length us, event | category | flops | bytes accessed | tf_op | source)
XLA Modules:
  0.0 137.5 jit_solution(1425654978176864140)
XLA Ops:
  3.2 131.6 %whole_kernel.1 = (f32[1,1536]{1,0:T(1,128)}, f32[768,384]{1,0:T(8,128)}, f32[6,128,384]{2,1,0:T(8,128)}) custom-call(f32[1]{0:T(128)S(6)} %copy.13.shift_ref, f32[1]{0:T(128)S(6)} %copy.14.scale_ref, s32[1]{0:T(128)S(6)} %copy.15.flag_ref, s32[1]{0:T(128)S(6)} %copy.12.count_ref, f32[1,1536]{1,0:T(1,128)} %weights_ref.1, s32[8,128]{1,0:T(8,128)} %bitcast.9, ...), custom_call_target="tpu_custom_call" | custom-call | flops 10066329600 | bytes 16777216 | tf_op jit(solution)/shard_map/whole_kernel/pallas_call | solution.py:622
  134.8 2.7 %keep_kernel.1 = (f32[1,1536]{1,0:T(1,128)}, f32[768,384]{1,0:T(8,128)}, f32[768,384]{1,0:T(8,128)}) custom-call(f32[1,1536]{1,0:T(1,128)} %get-tuple-element.6.refs_0_, f32[768,384]{1,0:T(8,128)} %get-tuple-element.7.refs_1_, f32[768,384]{1,0:T(8,128)} %bitcast.5), custom_call_target="tpu_custom_call" | custom-call | tf_op jit(solution)/shard_map/keep_kernel/pallas_call | solution.py:714

commit v7 on v6

--- a/solution.py
+++ b/solution.py
@@ -36,7 +36,7 @@
 
 CHUNK = 256
 STEPS = 32767.0
-JOBS = ((0, 0, 192), (0, 192, 192), (3, 0, 384), (1, 0, 384), (2, 0, 256), (2, 256, 128))
+JOBS = ((0, 64, 160), (0, 224, 160), (3, 64, 320), (1, 64, 320), (2, 64, 192), (2, 256, 128))
 
 
 def greet_all(me):
@@ -44,9 +44,9 @@
 
     @pl.loop(1, DEVICES, unroll=8)
     def _(step):
-        there = lax.rem(me + step, DEVICES)
+        there = (me + step) & (DEVICES - 1)
         pl.semaphore_signal(
-            barrier, inc=1, device_id=(there // COLS, lax.rem(there, COLS)), device_id_type=MESH
+            barrier, inc=1, device_id=(there >> 4, there & (COLS - 1)), device_id_type=MESH
         )
 
     return barrier
@@ -100,6 +100,8 @@
     got_most_ref,
     give_ref,
     got_ref,
+    early_ref,
+    late_ref,
     piece_ref,
     cols_ref,
     total_ref,
@@ -120,6 +122,10 @@
     row_recv,
     y_send,
     y_recv,
+    early_send,
+    early_recv,
+    late_send,
+    late_recv,
     save_sem,
     col_send,
     col_recv,
@@ -356,7 +362,11 @@
         own_ref[spot, :] = start.astype(jnp.bfloat16)
         for depth in (0, 1):
             lanes = [start[:, tile * TILE + depth * PART : tile * TILE + (depth + 1) * PART] for tile in range(BS)]
-            depth_ref[depth, spot, :] = jnp.concatenate(lanes, axis=1).astype(jnp.bfloat16)
+            halves = jnp.concatenate(lanes, axis=1).astype(jnp.bfloat16)
+            if tile_row == 0:
+                early_ref[depth, 0] = halves
+            else:
+                depth_ref[depth, spot, :] = halves
 
     z, core = row // 2, lax.rem(row, 2)
     x, y = col // RING, lax.rem(col, RING)
@@ -378,9 +388,10 @@
 
     def y_copy(dy):
         step = -dy
+        spot = pl.ds(PART, piece_rows - PART)
         return pltpu.make_async_remote_copy(
-            src_ref=depth_ref.at[side if dy == 2 else other],
-            dst_ref=piece_ref.at[0, dy],
+            src_ref=depth_ref.at[side if dy == 2 else other, spot],
+            dst_ref=piece_ref.at[0, dy, spot],
             send_sem=y_send.at[dy],
             recv_sem=y_recv.at[dy],
             device_id=device("y", step),
@@ -399,6 +410,28 @@
             send_sem=row_send.at[job, dx, part],
             recv_sem=row_recv.at[job, dx, part],
             device_id=device("x", step),
+            device_id_type=MESH,
+        )
+
+    def early_copy(dx, part=0):
+        step, source = hop((dx, part))
+        kinds = pl.ds(part, 1) if dx == 2 else pl.ds(0, 2)
+        return pltpu.make_async_remote_copy(
+            src_ref=early_ref.at[kinds, source],
+            dst_ref=early_ref.at[kinds, dx],
+            send_sem=early_send.at[dx, part],
+            recv_sem=early_recv.at[dx, part],
+            device_id=device("x", step),
+            device_id_type=MESH,
+        )
+
+    def late_copy(dy):
+        return pltpu.make_async_remote_copy(
+            src_ref=early_ref.at[side if dy == 2 else other],
+            dst_ref=late_ref.at[dy],
+            send_sem=late_send.at[dy],
+            recv_sem=late_recv.at[dy],
+            device_id=device("y", -dy),
             device_id_type=MESH,
         )
 
@@ -449,6 +482,8 @@
         for part in (0, 1):
             x_copy(job, 2, part).wait_recv()
 
+    for dx in (3, 1):
+        go(early_copy(dx))
     start_job(0)
     start_job(1)
     for dy in (3, 1, 2):
@@ -464,7 +499,7 @@
         return jnp.concatenate(found, axis=1)
 
     for tile_row in range(BS):
-        give_ref[tile_row] = strip(tile_row, other)
+        give_ref[tile_row] = strip(tile_row, other).astype(jnp.bfloat16)
     pair = pltpu.make_async_remote_copy(
         src_ref=give_ref,
         dst_ref=got_ref,
@@ -476,6 +511,9 @@
     for tile_row in range(BS):
         xc_ref[pl.ds(pl.multiple_of(tile_row * TILE + side * PART, PART), PART), :] = strip(tile_row, side)
 
+    for dx, part in ((3, 0), (1, 1)):
+        early_copy(dx).wait_recv()
+        go(early_copy(2, part))
     pass_on(0)
     y_copy(3).wait_recv()
     start_job(2)
@@ -486,6 +524,10 @@
         z_copy(dz).wait_recv()
         go(z_copy(2, part))
         go(core_copy(dz))
+    for part in (0, 1):
+        early_copy(2, part).wait_recv()
+    for dy in (3, 1, 2):
+        go(late_copy(dy))
     y_copy(2).wait_recv()
     go(pair)
     pass_on(2)
@@ -505,6 +547,19 @@
             total_ref[group, spot, :] = product
         else:
             total_ref[group, spot, :] += product
+
+    def multiply_early(dy):
+        group = dy % 2
+        spot = pl.ds(0, PART)
+        for dx in range(RING):
+            there_x, there_y = turn(x, dx), turn(y, dy)
+            factor = cols_ref[there_x, there_y // 2]
+            values = early_ref[side, dx] if dy == 0 else late_ref[dy, dx]
+            product = jnp.dot(values, factor, preferred_element_type=jnp.float32)
+            if dx == 0 and dy in (0, 3):
+                total_ref[group, spot, :] = product
+            else:
+                total_ref[group, spot, :] += product
 
     cuts = ((1, 0, 384), (0, 0, 256), (0, 256, 128))
 
@@ -544,7 +599,7 @@
                 down = lax.broadcasted_iota(jnp.int32, (PART, half_wide), 0) + (row * wide + first)
                 across = lax.broadcasted_iota(jnp.int32, (PART, half_wide), 1) + col * half_wide
                 shift = jnp.where(down == across, shift_ref[0], jnp.float32(0.0))
-                start = shift + scale_ref[0] * (core_ref[tile_row, far_part] + got_ref[tile_row])
+                start = shift + scale_ref[0] * (core_ref[tile_row, far_part] + got_ref[tile_row].astype(jnp.float32))
             square = total_ref[group, spot, near_cols] + got_total_ref[kind, spot, :].astype(jnp.float32)
             out_ref[tile_row, kind_part] = sign * square + twice * start
         tile_rows = pl.ds(first_row // PART, count // PART)
@@ -575,13 +630,19 @@
         multiply(3, dx)
     far_landed(3)
     multiply(3, 2)
+    for dy in (3, 1):
+        late_copy(dy).wait_recv()
+        multiply_early(dy)
     hand_over(0)
     pass_on(4)
+    multiply_early(0)
+    late_copy(2).wait_recv()
+    multiply_early(2)
     for dx in (0, 3, 1):
         multiply(4, dx)
     pair.wait_recv()
     for tile_row in range(BS):
-        xc_ref[pl.ds(pl.multiple_of(tile_row * TILE + other * PART, PART), PART), :] = got_ref[tile_row]
+        xc_ref[pl.ds(pl.multiple_of(tile_row * TILE + other * PART, PART), PART), :] = got_ref[tile_row].astype(jnp.float32)
     save_xc = pltpu.make_async_copy(xc_ref, xc_hbm, load_sem.at[1])
     save_xc.start()
     multiply(5, 0)
@@ -654,8 +715,10 @@
             pltpu.VMEM((BS, PART, wide), jnp.int16),
             pltpu.VMEM((8, TILE), f32),
             pltpu.VMEM((8, TILE), f32),
-            pltpu.VMEM((BS, PART, wide), f32),
-            pltpu.VMEM((BS, PART, wide), f32),
+            pltpu.VMEM((BS, PART, wide), bf16),
+            pltpu.VMEM((BS, PART, wide), bf16),
+            pltpu.VMEM((2, RING, PART, wide), bf16),
+            pltpu.VMEM((RING, RING, PART, wide), bf16),
             pltpu.VMEM((RING, RING, BS * PART, wide), bf16),
             pltpu.VMEM((RING, 2, BS * PART, 2 * wide), bf16),
             pltpu.VMEM((2, BS * PART, 2 * wide), f32),
@@ -676,6 +739,10 @@
             dma((len(JOBS), RING, 2)),
             dma((RING,)),
             dma((RING,)),
+            dma((RING, 2)),
+            dma((RING, 2)),
+            dma((RING,)),
+            dma((RING,)),
             dma((4,)),
             dma((RING, 2)),
             dma((RING, 2)),
@@ -698,8 +765,12 @@
     loads, saves = [], []
     for i in range(count):
         source, target, held = refs[i], refs[count + i], refs[2 * count + i]
-        loads.append(pltpu.make_async_copy(source, held, sems.at[0, i]))
-        saves.append(pltpu.make_async_copy(held, target, sems.at[1, i]))
+        parts = 4 if source.shape[0] > 1 else 1
+        size = source.shape[0] // parts
+        for part in range(parts):
+            spot = pl.ds(part * size, size)
+            loads.append(pltpu.make_async_copy(source.at[spot], held.at[spot], sems.at[0, i, part]))
+            saves.append(pltpu.make_async_copy(held.at[spot], target.at[spot], sems.at[1, i, part]))
     for load in loads:
         load.start()
     for load, save in zip(loads, saves):
@@ -717,7 +788,7 @@
         out_shape=tuple(jax.ShapeDtypeStruct(a.shape, a.dtype) for a in arrays),
         in_specs=[hbm] * len(arrays),
         out_specs=(hbm,) * len(arrays),
-        scratch_shapes=[pltpu.VMEM(a.shape, a.dtype) for a in arrays] + [pltpu.SemaphoreType.DMA((2, len(arrays)))],
+        scratch_shapes=[pltpu.VMEM(a.shape, a.dtype) for a in arrays] + [pltpu.SemaphoreType.DMA((2, len(arrays), 4))],
     )(*arrays)
 
 

time: 138 us -> 135 us (0.978)
  Pallas kernels: 134 us -> 132 us
    pallas_call x1, Pallas kernels: 132 us -> 129 us  [whole(): pl.pallas_call(whole_kernel, name='whole_kernel', out_shape=(jax.ShapeDty...]
where the time goes in v7:
time: 135 us
  Pallas kernels  132 us (98%)
  between operations  3.22 us (2%)
    pallas_call x1, Pallas kernels, whole(): pl.pallas_call(whole_kernel, name='whole_kernel', out_shape=(jax.ShapeDty...  129 us

profile of v7, /device:TPU:0, one launch (start us, length us, event | category | flops | bytes accessed | tf_op | source)
XLA Modules:
  0.0 135.0 jit_solution(15624360840648985108)
XLA Ops:
  3.2 129.2 %whole_kernel.1 = (f32[1,1536]{1,0:T(1,128)}, f32[768,384]{1,0:T(8,128)}, f32[6,128,384]{2,1,0:T(8,128)}) custom-call(f32[1]{0:T(128)S(6)} %copy.13.shift_ref, f32[1]{0:T(128)S(6)} %copy.14.scale_ref, s32[1]{0:T(128)S(6)} %copy.15.flag_ref, s32[1]{0:T(128)S(6)} %copy.12.count_ref, f32[1,1536]{1,0:T(1,128)} %weights_ref.1, s32[8,128]{1,0:T(8,128)} %bitcast.9, ...), custom_call_target="tpu_custom_call" | custom-call | flops 10066329600 | bytes 16777216 | tf_op jit(solution)/shard_map/whole_kernel/pallas_call | solution.py:683
  132.4 2.6 %keep_kernel.1 = (f32[1,1536]{1,0:T(1,128)}, f32[768,384]{1,0:T(8,128)}, f32[768,384]{1,0:T(8,128)}) custom-call(f32[1,1536]{1,0:T(1,128)} %get-tuple-element.6.refs_0_, f32[768,384]{1,0:T(8,128)} %get-tuple-element.7.refs_1_, f32[768,384]{1,0:T(8,128)} %bitcast.5), custom_call_target="tpu_custom_call" | custom-call | tf_op jit(solution)/shard_map/keep_kernel/pallas_call | solution.py:785

commit v8 on v7

--- a/solution.py
+++ b/solution.py
@@ -218,7 +218,7 @@
 
     for half in (0, 1):
 
-        @pl.loop(1 - half, DEVICES // 2)
+        @pl.loop(1 - half, DEVICES // 2, unroll=4)
         def _(count, half=half):
             target = offset_device(row, col, half, count)
             batch = stage(target)
@@ -315,7 +315,7 @@
         for which in (0, 1):
             block_ref[bands[which], :] = result[which * 2 * TILE : (which + 1) * 2 * TILE]
 
-        @pl.loop(1 - half, DEVICES // 2)
+        @pl.loop(1 - half, DEVICES // 2, unroll=4)
         def _(count, half=half):
             target = offset_device(row, col, half, count)
             pltpu.make_async_remote_copy(
@@ -338,7 +338,7 @@
     save_rho.start()
     pltpu.make_async_copy(landed_ref, landed_ref, all_recv.at[1]).wait()
 
-    @pl.loop(0, DEVICES)
+    @pl.loop(0, DEVICES, unroll=4)
     def _(batch):
         sums_ref[batch] = sums_ref[chain_ref[0, batch]] + landed_ref[batch].astype(jnp.float32)
 

time: 135 us -> 135 us (level)
  no operation moved by 1% of the time
where the time goes in v8:
time: 135 us
  Pallas kernels  131 us (97%)
  between operations  3.22 us (2%)
    pallas_call x1, Pallas kernels, whole(): pl.pallas_call(whole_kernel, name='whole_kernel', out_shape=(jax.ShapeDty...  129 us

profile of v8, /device:TPU:0, one launch (start us, length us, event | category | flops | bytes accessed | tf_op | source)
XLA Modules:
  0.0 134.6 jit_solution(14411920621525125918)
XLA Ops:
  3.2 128.8 %whole_kernel.1 = (f32[1,1536]{1,0:T(1,128)}, f32[768,384]{1,0:T(8,128)}, f32[6,128,384]{2,1,0:T(8,128)}) custom-call(f32[1]{0:T(128)S(6)} %copy.13.shift_ref, f32[1]{0:T(128)S(6)} %copy.14.scale_ref, s32[1]{0:T(128)S(6)} %copy.15.flag_ref, s32[1]{0:T(128)S(6)} %copy.12.count_ref, f32[1,1536]{1,0:T(1,128)} %weights_ref.1, s32[8,128]{1,0:T(8,128)} %bitcast.9, ...), custom_call_target="tpu_custom_call" | custom-call | flops 10066329600 | bytes 16777216 | tf_op jit(solution)/shard_map/whole_kernel/pallas_call | solution.py:683
  132.1 2.6 %keep_kernel.1 = (f32[1,1536]{1,0:T(1,128)}, f32[768,384]{1,0:T(8,128)}, f32[768,384]{1,0:T(8,128)}) custom-call(f32[1,1536]{1,0:T(1,128)} %get-tuple-element.6.refs_0_, f32[768,384]{1,0:T(8,128)} %get-tuple-element.7.refs_1_, f32[768,384]{1,0:T(8,128)} %bitcast.5), custom_call_target="tpu_custom_call" | custom-call | tf_op jit(solution)/shard_map/keep_kernel/pallas_call | solution.py:785
